TPU v7x, 32 devices: a whole 2x2x4 slice. The times are simulated.
32 devices in a mesh: row: 4 (over y, core), col: 8 (over z, x).
Axes of the slice: x: 2, y: 2, z: 4, core: 2. Of those that a mesh axis runs over, the one named last changes fastest.
Arguments:
- atoms: bfloat16 [4096, 128], P(('row', 'col')), may hold values from -6 to 6
- atom_pair: bfloat16 [128, 16, 32, 128], P(('row', 'col')), may hold values from -6 to 6
- atom_token: int32 [4096], P(('row', 'col')), may hold values from 0 to 1023, as said below
- single: bfloat16 [1024, 768], P('row'), may hold values from -6 to 6
- pair: bfloat16 [1024, 1024, 128], P('row', 'col'), may hold values from -6 to 6
- atom_w: bfloat16 [128, 4, 128], replicated, may hold values from -0.5 to 0.5
- atom_pair_w: bfloat16 [16, 4], replicated, may hold values from -24 to 24
- atom_wo: bfloat16 [128, 128], replicated, may hold values from -0.5 to 0.5
- agg_w: bfloat16 [128, 768], replicated, may hold values from -0.5 to 0.5
- trans_in: bfloat16 [128, 2, 256], replicated, may hold values from -0.5 to 0.5
- trans_out: bfloat16 [256, 128], replicated, may hold values from -0.375 to 0.375
- bias_w: bfloat16 [128, 16], replicated, may hold values from -6 to 6
- token_w: bfloat16 [768, 4, 768], P(None, None, 'col'), may hold values from -0.21875 to 0.21875
- token_wo: bfloat16 [768, 768], P('col'), may hold values from -0.21875 to 0.21875
- back_w: bfloat16 [768, 128], P('col'), may hold values from -0.21875 to 0.21875
Outputs:
- single_out: bfloat16 [1024, 768], P('row', 'col')
- atoms_out: bfloat16 [4096, 128], P(('row', 'col'))
Inputs may be any that keep to these rules, and one draw needn't show every extreme that they name: `atom_token`: atoms are in token order; the 1024 atoms of block b (b from 0) belong to tokens b * 256 to (b + 1) * 256 - 1; every token has 1 to 7 atoms, and in every block some token has exactly 7.
All inputs are finite; a program needn't handle non-finite values.
Results may differ from a plain program's by a relative error of at most 0.024.
The roundings to bfloat16 on the way count: a program that leaves them out, or rounds other values in their place, can miss the bound.
Values may be sent and summed in bfloat16 or wider, within the bound.
A program may use at most 64 MiB of HBM per device.

v0:
```python
import math

import jax
import jax.numpy as jnp
from jax import lax
from jax.sharding import PartitionSpec as P

HEADS = 16
HEAD = 48
CA = 128
ATOM_HEADS = 4
ATOM_HEAD = 32
QW = 32
KW = 128


epsilon = 1e-05
masked_score = -1e30


def extended_2(value, sides, width):
    for axis, dim in sides:
        size, length = (lax.axis_size(axis), value.shape[dim])
        up = [(i, (i + 1) % size) for i in range(size - 1)]
        down = [(j, i) for i, j in up]
        last = lax.slice_in_dim(value, length - width, length, axis=dim)
        initial = lax.slice_in_dim(value, 0, width, axis=dim)
        before = lax.ppermute(last, axis, up)
        after = lax.ppermute(initial, axis, down)
        value = jnp.concatenate([before, value, after], axis=dim)
    return value


def layer_norm(values):
    centred = values - jnp.mean(values, axis=-1, keepdims=True)
    spread = jnp.mean(centred * centred, axis=-1, keepdims=True)
    return centred * lax.rsqrt(spread + epsilon)


def rounded(values):
    return lax.optimization_barrier(values.astype(jnp.bfloat16))


def softmax_rows(scores):
    highest = jnp.max(scores, axis=-1, keepdims=True)
    raised = jnp.exp(scores - highest)
    return (raised / jnp.sum(raised, axis=-1, keepdims=True)).astype(jnp.bfloat16)


def pair_block(tile, trans_in, trans_out, bias_w):
    normed = layer_norm(tile.astype(jnp.float32)).astype(jnp.bfloat16)
    both = jnp.einsum("ijc,cmf->ijmf", normed, trans_in, preferred_element_type=jnp.float32)
    hidden = (jax.nn.silu(both[:, :, 0, :]) * both[:, :, 1, :]).astype(jnp.bfloat16)
    update = jnp.einsum("ijf,fc->ijc", hidden, trans_out, preferred_element_type=jnp.float32)
    renewed = rounded(tile.astype(jnp.float32) + update)
    renormed = layer_norm(renewed.astype(jnp.float32)).astype(jnp.bfloat16)
    return jnp.einsum("ijc,ch->hij", renormed, bias_w, preferred_element_type=jnp.float32).astype(
        jnp.bfloat16
    )


def body(
    atoms,
    atom_pair,
    atom_token,
    single,
    pair,
    atom_w,
    atom_pair_w,
    atom_wo,
    agg_w,
    trans_in,
    trans_out,
    bias_w,
    token_w,
    token_wo,
    back_w,
):
    atom_count = atoms.shape[0]
    windows = atom_count // QW
    rim = (KW - QW) // 2
    atom_norm = layer_norm(atoms.astype(jnp.float32)).astype(jnp.bfloat16)
    projected = jnp.einsum(
        "ac,cmd->amd", atom_norm, atom_w, preferred_element_type=jnp.float32
    ).astype(jnp.bfloat16)
    extended = extended_2(atoms, ((("row", "col"), 0),), rim)
    ext_norm = layer_norm(extended.astype(jnp.float32)).astype(jnp.bfloat16)
    key_value = jnp.einsum(
        "ac,cmd->amd", ext_norm, atom_w[:, 1:3, :], preferred_element_type=jnp.float32
    ).astype(jnp.bfloat16)
    device = lax.axis_index(("row", "col"))
    all_atoms = atom_count * lax.axis_size(("row", "col"))
    positions = device * atom_count - rim + jnp.arange(atom_count + 2 * rim)
    inside = (positions >= 0) & (positions < all_atoms)
    window_keys = jnp.stack(
        [
            lax.slice_in_dim(key_value, window * QW, window * QW + KW, axis=0)
            for window in range(windows)
        ]
    )
    window_mask = jnp.stack(
        [
            lax.slice_in_dim(inside, window * QW, window * QW + KW, axis=0)
            for window in range(windows)
        ]
    )
    queries = projected[:, 0, :].reshape(windows, QW, ATOM_HEADS, ATOM_HEAD)
    key_part = window_keys[:, :, 0, :].reshape(windows, KW, ATOM_HEADS, ATOM_HEAD)
    value_part = window_keys[:, :, 1, :].reshape(windows, KW, ATOM_HEADS, ATOM_HEAD)
    atom_bias = jnp.einsum(
        "wcij,ch->whij", atom_pair, atom_pair_w, preferred_element_type=jnp.float32
    )
    scores = (
        jnp.einsum("wiha,wjha->whij", queries, key_part, preferred_element_type=jnp.float32)
        / math.sqrt(ATOM_HEAD)
        + atom_bias
    )
    scores = jnp.where(window_mask[:, None, None, :], scores, masked_score)
    weights = softmax_rows(scores)
    attended = jnp.einsum(
        "whij,wjha->wiha", weights, value_part, preferred_element_type=jnp.float32
    ).reshape(atom_count, CA)
    gated = (jax.nn.sigmoid(projected[:, 3, :].astype(jnp.float32)) * attended).astype(jnp.bfloat16)
    atoms_mid = rounded(
        atoms.astype(jnp.float32) + jnp.dot(gated, atom_wo, preferred_element_type=jnp.float32)
    )
    query_rows = single.shape[0]
    row_start = lax.axis_index("row") * query_rows
    within = atom_token - row_start
    onehot = (jnp.arange(query_rows)[:, None] == within[None, :]).astype(jnp.bfloat16)
    features = jax.nn.relu(jnp.dot(atoms_mid, agg_w, preferred_element_type=jnp.float32)).astype(
        jnp.bfloat16
    )
    token_part = jnp.dot(onehot, features, preferred_element_type=jnp.float32)
    count_part = jnp.sum(onehot.astype(jnp.float32), axis=1)
    token_sum, token_count = (
        lax.psum(token_part.astype(jnp.bfloat16), "col").astype(jnp.float32),
        lax.psum(count_part.astype(jnp.bfloat16), "col").astype(jnp.float32),
    )
    token_in = rounded(single.astype(jnp.float32) + token_sum / token_count[:, None])
    key_cols = pair.shape[1]
    blocks = pair.reshape(query_rows // 16, 16, key_cols, pair.shape[2])
    bias_blocks = lax.map(lambda tile: pair_block(tile, trans_in, trans_out, bias_w), blocks)
    pair_bias = jnp.moveaxis(bias_blocks, 1, 0).reshape(HEADS, query_rows, key_cols)
    token_norm = layer_norm(token_in.astype(jnp.float32)).astype(jnp.bfloat16)
    token_proj = jnp.einsum(
        "td,dme->tme", token_norm, token_w, preferred_element_type=jnp.float32
    ).astype(jnp.bfloat16)
    head_cols = token_w.shape[2]
    kv_rows = lax.all_gather(token_proj[:, 1:3, :], "row", axis=0, tiled=True)
    all_tokens = kv_rows.shape[0]
    bias_rows = lax.all_to_all(pair_bias, "col", split_axis=0, concat_axis=2, tiled=True)
    heads_here = head_cols // HEAD
    query_part = token_proj[:, 0, :].reshape(query_rows, heads_here, HEAD)
    token_keys = kv_rows[:, 0, :].reshape(all_tokens, heads_here, HEAD)
    token_values = kv_rows[:, 1, :].reshape(all_tokens, heads_here, HEAD)
    token_scores = jnp.einsum(
        "ihe,jhe->hij", query_part, token_keys, preferred_element_type=jnp.float32
    ) / math.sqrt(HEAD)
    token_weights = softmax_rows(token_scores + bias_rows.astype(jnp.float32))
    token_attn = jnp.einsum(
        "hij,jhe->ihe", token_weights, token_values, preferred_element_type=jnp.float32
    ).reshape(query_rows, head_cols)
    token_gated = (jax.nn.sigmoid(token_proj[:, 3, :].astype(jnp.float32)) * token_attn).astype(
        jnp.bfloat16
    )
    own_cols = token_wo.shape[0]
    own_input = lax.dynamic_slice_in_dim(token_in, lax.axis_index("col") * own_cols, own_cols, 1)
    projection = lax.psum_scatter(
        jnp.dot(token_gated, token_wo, preferred_element_type=jnp.float32).astype(jnp.bfloat16),
        "col",
        scatter_dimension=1,
        tiled=True,
    ).astype(jnp.float32)
    single_out = (own_input.astype(jnp.float32) + projection).astype(jnp.bfloat16)
    back_sum = lax.psum(
        jnp.dot(single_out, back_w, preferred_element_type=jnp.float32).astype(jnp.bfloat16), "col"
    )
    picked = jnp.einsum("ta,tc->ac", onehot, back_sum, preferred_element_type=jnp.float32)
    atoms_out = (atoms_mid.astype(jnp.float32) + picked).astype(jnp.bfloat16)
    return (single_out, atoms_out)


def solution(mesh):
    in_specs = (
        P(("row", "col"), None),
        P(("row", "col"), None, None, None),
        P(("row", "col")),
        P("row", None),
        P("row", "col", None),
        P(),
        P(),
        P(),
        P(),
        P(),
        P(),
        P(),
        P(None, None, "col"),
        P("col", None),
        P("col", None),
    )
    out_specs = (P("row", "col"), P(("row", "col"), None))
    return jax.shard_map(body, mesh=mesh, in_specs=in_specs, out_specs=out_specs, check_vma=False)
```

profile of v0, /device:TPU:0, one launch (start us, length us, event | category | flops | bytes accessed | tf_op | source)
XLA Modules:
  0.0 362.9 jit_solution(5206316018700947744)
XLA Ops:
  8.0 4.8 %collective-permute-start = (bf16[48,128]{1,0:T(8,128)(2,1)S(1)}, bf16[48,128]{1,0:T(8,128)(2,1)S(1)}, u32[]{:S(2)}, u32[]{:S(2)}) collective-permute-start(bf16[48,128]{1,0:T(8,128)(2,1)S(1)} %get-tuple-element.87), channel_id=1, source_target_pairs={{0,1},{1,2},{2,3},{3,4},{4,5},{5,6},{6,7},{7,8},{8,9},{9,10},{10,1... | collective-permute-start | bytes 36872 | tf_op jit(solution)/shard_map/ppermute | solution.py:28
  26.9 135.3 %while.10 = (s32[]{:T(128)}, bf16[16,16,16,128]{3,1,2,0:T(8,128)(2,1)S(1)}, bf16[16,16,128,128]{3,2,1,0:T(8,128)(2,1)}, bf16[128,2,256]{2,0,1:T(8,128)(2,1)S(1)}...) while((s32[]{:T(128)}, bf16[16,16,16,128]{3,1,2,0:T(8,128)(2,1)S(1)}, ...), condition=%wide.region_16.17_spmd, body=%wide.region_11.16_spmd.sunk | while | flops 420253696 | bytes 12997213 | solution.py:143
  29.9 2.0 fusion.126
  38.3 2.0 fusion.126
  46.8 2.0 fusion.126
  55.2 2.0 fusion.126
  63.7 2.0 fusion.126
  72.2 2.0 fusion.126
  80.6 2.0 fusion.126
  89.1 2.0 fusion.126
  97.6 2.0 fusion.126
  106.0 2.0 fusion.126
  114.5 2.0 fusion.126
  122.9 2.0 fusion.126
  131.4 2.0 fusion.126
  139.8 2.0 fusion.126
  148.3 2.0 fusion.126
  156.7 2.0 fusion.126
  163.5 7.0 %all-to-all-start = ((bf16[16,256,128]{2,1,0:T(8,128)(2,1)}), bf16[16,256,128]{2,1,0:T(8,128)(2,1)S(1)}, u32[]{:S(2)}, u32[]{:S(2)}) async-start(bf16[16,256,128]{2,1,0:T(8,128)(2,1)} %bitcast.35), calls=%async_computation | async-start | bytes 2097152 | tf_op jit(solution)/shard_map/all_to_all | solution.py:152
  170.6 33.9 %psum.22 = bf16[256]{0:T(256)(128)(2,1)S(1)} all-reduce(bf16[256]{0:T(256)(128)(2,1)S(1)} %fusion.63), channel_id=1, replica_groups=mesh['row'=4,'col'=8] {'col'}, use_global_device_ids=true, to_apply=%region_8.9 | all-reduce | flops 256 | bytes 1024 | tf_op jit(solution)/shard_map/psum | solution.py:138
  206.7 6.1 %all_gather.3 = bf16[1024,2,96]{0,2,1:T(8,128)(2,1)S(1)} all-gather(bf16[256,2,96]{0,2,1:T(8,128)(2,1)S(1)} %slice.98), channel_id=1, replica_groups=mesh['row'=4,'col'=8] {'row'}, dimensions={0}, use_global_device_ids=true | all-gather | bytes 491520 | tf_op jit(solution)/shard_map/all_gather | solution.py:150
  219.9 2.0 fusion.32
  222.0 61.5 %reduce-scatter.4.cloned.1.call-done = bf16[96,256]{1,0:T(8,128)(2,1)} async-done(((bf16[768,256]{1,0:T(8,128)(2,1)}), bf16[96,256]{1,0:T(8,128)(2,1)}) %reduce-scatter.4.cloned.1.call-update) | async-done | bytes 49168
  286.0 68.8 %all-reduce.5.cloned.1.call-done = bf16[256,128]{1,0:T(8,128)(2,1)} async-done(((bf16[256,128]{1,0:T(8,128)(2,1)}), bf16[256,128]{1,0:T(8,128)(2,1)}) %all-reduce.5.cloned.1.call-update) | async-done | bytes 65552 | tf_op jit(solution)/shard_map/psum | solution.py:176
  (250 shorter events, 131.4 us)
Async XLA Ops:
  7.2 199.0 %copy-start = (bf16[768,4,96]{0,2,1:T(8,128)(2,1)S(1)}, bf16[768,4,96]{0,2,1:T(8,128)(2,1)}, u32[]{:S(2)}) copy-start(bf16[768,4,96]{0,2,1:T(8,128)(2,1)} %param.29) | copy-start | bytes 1769476
  7.2 15.9 %copy-start.2 = (bf16[128,128]{1,0:T(8,128)(2,1)S(1)}, bf16[128,128]{1,0:T(8,128)(2,1)}, u32[]{:S(2)}) copy-start(bf16[128,128]{1,0:T(8,128)(2,1)} %param.17) | copy-start | bytes 98308
  7.2 197.3 %all-reduce.3.cloned.1.call-start = ((), (), s32[]{:S(2)}) async-start(), calls=%async_computation.2 | async-start | bytes 786432 | tf_op jit(solution)/shard_map/psum | solution.py:137
  8.0 13.2 %collective-permute-start = (bf16[48,128]{1,0:T(8,128)(2,1)S(1)}, bf16[48,128]{1,0:T(8,128)(2,1)S(1)}, u32[]{:S(2)}, u32[]{:S(2)}) collective-permute-start(bf16[48,128]{1,0:T(8,128)(2,1)S(1)} %get-tuple-element.87), channel_id=1, source_target_pairs={{0,1},{1,2},{2,3},{3,4},{4,5},{5,6},{6,7},{7,8},{8,9},{9,10},{10,1... | collective-permute-start | bytes 36872 | tf_op jit(solution)/shard_map/ppermute | solution.py:28
  12.9 8.4 %collective-permute-start.1 = (bf16[48,128]{1,0:T(8,128)(2,1)S(1)}, bf16[48,128]{1,0:T(8,128)(2,1)S(1)}, u32[]{:S(2)}, u32[]{:S(2)}) collective-permute-start(bf16[48,128]{1,0:T(8,128)(2,1)S(1)} %get-tuple-element.88), channel_id=1, source_target_pairs={{1,0},{2,1},{3,2},{4,3},{5,4},{6,5},{7,6},{8,7},{9,8},{10,9},{11,1... | collective-permute-start | bytes 36872 | tf_op jit(solution)/shard_map/ppermute | solution.py:29
  19.2 151.3 %copy-start.7 = (s32[128]{0:T(128)}, s32[128]{0:T(128)S(1)}, u32[]{:S(2)}) copy-start(s32[128]{0:T(128)S(1)} %broadcast_subtract_fusion) | copy-start | bytes 1540
  23.4 2.1 copy-start.10
  23.5 2.2 copy-start.4
  23.8 3.1 copy-start.9
  23.8 3.1 copy-start.11
  162.2 42.3 %copy-start.3 = (bf16[256,768]{1,0:T(8,128)(2,1)S(1)}, bf16[256,768]{1,0:T(8,128)(2,1)}, u32[]{:S(2)}) copy-start(bf16[256,768]{1,0:T(8,128)(2,1)} %param.20) | copy-start | bytes 1179652
  163.5 50.0 %all-to-all-start = ((bf16[16,256,128]{2,1,0:T(8,128)(2,1)}), bf16[16,256,128]{2,1,0:T(8,128)(2,1)S(1)}, u32[]{:S(2)}, u32[]{:S(2)}) async-start(bf16[16,256,128]{2,1,0:T(8,128)(2,1)} %bitcast.35), calls=%async_computation | async-start | bytes 2097152 | tf_op jit(solution)/shard_map/all_to_all | solution.py:152
  170.5 112.9 %reduce-scatter.4.cloned.1.call-start = ((), (), s32[]{:S(2)}) async-start(), calls=%async_computation.4 | async-start | bytes 442368
  213.5 1.0 copy-start.1
  216.2 0.9 copy-start.5
  217.1 67.3 %copy-start.6 = (bf16[96,128]{1,0:T(8,128)(2,1)S(1)}, bf16[96,128]{1,0:T(8,128)(2,1)}, u32[]{:S(2)}) copy-start(bf16[96,128]{1,0:T(8,128)(2,1)} %param.31) | copy-start | bytes 73732
  217.1 137.6 %copy-start.8 = (s32[128]{0:T(128)S(1)}, s32[128]{0:T(128)}, u32[]{:S(2)}) copy-start(s32[128]{0:T(128)} %copy-done.7) | copy-start | bytes 1540
  221.9 132.8 %all-reduce.5.cloned.1.call-start = ((), (), s32[]{:S(2)}) async-start(), calls=%async_computation.3 | async-start | bytes 131072 | tf_op jit(solution)/shard_map/psum | solution.py:176
Sparse Core Ops, SparseCore 0:
  27.0 73.7 all-reduce.2
  222.0 61.3 reduce-scatter.3
  287.2 67.4 all-reduce.4
where the time goes:
time: 366 us; the launch traced here: 363 us
  waiting for transfers between devices  130 us (36%)
  matrix products  86.9 us (24%)
  other arithmetic  68.5 us (19%)
  blocking collectives  40 us (11%)
  between operations  14.2 us (4%)
  starting transfers between devices  13.2 us (4%)
  local copies, waits for them, and re-layouts  8.57 us (2%)
    psum x1, waiting for transfers between devices, body(): lax.psum(jnp.dot(single_out, back_w, preferred_element_type=jnp.float32)....  68.8 us
    unnamed x4, waiting for transfers between devices  61.5 us
    reduce_sum x35, other arithmetic, layer_norm(): spread = jnp.mean(centred * centred, axis=-1, keepdims=True)  39 us
    psum x1, blocking collectives, body(): lax.psum(count_part.astype(jnp.bfloat16), 'col').astype(jnp.float32)  33.9 us
    dot_general x16, matrix products, pair_block(): jnp.einsum('ijc,cmf->ijmf', normed, trans_in, preferred_element_type=jnp....  32.1 us
    dot_general x16, matrix products, pair_block(): jnp.einsum('ijf,fc->ijc', hidden, trans_out, preferred_element_type=jnp.f...  29.3 us
    reduce_sum x35, other arithmetic, layer_norm(): centred = values - jnp.mean(values, axis=-1, keepdims=True)  25.3 us
    dot_general x16, matrix products, pair_block(): jnp.einsum('ijc,ch->hij', renormed, bias_w, preferred_element_type=jnp.fl...  11.9 us
  transfers between devices with their start and end apart: 6, of which 2 were waited for; matrix products, arithmetic and copies ran while one was open for 40% of the time, Pallas kernels for 0%

commit v1 on v0

--- a/solution.py
+++ b/solution.py
@@ -1,13 +1,17 @@
+import functools
 import math
 
 import jax
 import jax.numpy as jnp
 from jax import lax
+from jax.experimental import pallas as pl
+from jax.experimental.pallas import tpu as pltpu
 from jax.sharding import PartitionSpec as P
 
 HEADS = 16
 HEAD = 48
 CA = 128
+CZ = 128
 ATOM_HEADS = 4
 ATOM_HEAD = 32
 QW = 32
@@ -47,16 +51,148 @@
     return (raised / jnp.sum(raised, axis=-1, keepdims=True)).astype(jnp.bfloat16)
 
 
-def pair_block(tile, trans_in, trans_out, bias_w):
-    normed = layer_norm(tile.astype(jnp.float32)).astype(jnp.bfloat16)
-    both = jnp.einsum("ijc,cmf->ijmf", normed, trans_in, preferred_element_type=jnp.float32)
-    hidden = (jax.nn.silu(both[:, :, 0, :]) * both[:, :, 1, :]).astype(jnp.bfloat16)
-    update = jnp.einsum("ijf,fc->ijc", hidden, trans_out, preferred_element_type=jnp.float32)
-    renewed = rounded(tile.astype(jnp.float32) + update)
-    renormed = layer_norm(renewed.astype(jnp.float32)).astype(jnp.bfloat16)
-    return jnp.einsum("ijc,ch->hij", renormed, bias_w, preferred_element_type=jnp.float32).astype(
-        jnp.bfloat16
-    )
+ROWS_STEP = 16
+ROWS_CHAIN = 2
+
+
+def pair_kernel(
+    peers, pair_ref, centre_ref, win_ref, wout_ref, bw_ref, out_ref,
+    stage, send, send_sem, recv_sem, own_sem,
+):
+    step = pl.program_id(0)
+    steps = pl.num_programs(0)
+    row, col = lax.axis_index("row"), lax.axis_index("col")
+    group = send.shape[0] // peers
+    width = pair_ref.shape[1]
+
+    def other(k):
+        return lax.rem(col + k, peers)
+
+    @pl.when(step == 0)
+    def _():
+        barrier = pltpu.get_barrier_semaphore()
+        for k in range(1, peers):
+            pl.semaphore_signal(
+                barrier, inc=1, device_id=(row, other(k)), device_id_type=pl.DeviceIdType.MESH
+            )
+        pl.semaphore_wait(barrier, peers - 1)
+
+    def first(k):
+        x = pair_ref[k * ROWS_CHAIN : (k + 1) * ROWS_CHAIN].reshape(ROWS_CHAIN * width, CZ)
+        both = lax.dot_general(
+            centre_ref[...], x, (((1,), (1,)), ((), ())), preferred_element_type=jnp.float32
+        )
+        centred = both[:CZ]
+        spread = jnp.mean(centred * centred, axis=0, keepdims=True)
+        normed = (centred * lax.rsqrt(spread + epsilon)).astype(jnp.bfloat16)
+        return centred, both[CZ : CZ + 1], normed
+
+    def second(state):
+        centred, average, normed = state
+        both = jnp.dot(win_ref[...], normed, preferred_element_type=jnp.float32)
+        half = both.shape[0] // 2
+        gate = both[:half]
+        hidden = ((gate + gate * jnp.tanh(gate)) * both[half:]).astype(jnp.bfloat16)
+        return centred + average, hidden
+
+    def third(state):
+        tile, hidden = state
+        update = jnp.dot(wout_ref[...], hidden, preferred_element_type=jnp.float32)
+        renewed = (tile + update).astype(jnp.bfloat16).astype(jnp.float32)
+        centred = renewed - jnp.mean(renewed, axis=0, keepdims=True)
+        spread = jnp.mean(centred * centred, axis=0, keepdims=True)
+        return (centred * lax.rsqrt(spread + epsilon)).astype(jnp.bfloat16)
+
+    def fourth(k, renormed):
+        bias = jnp.dot(bw_ref[...], renormed, preferred_element_type=jnp.float32)
+        for i in range(ROWS_CHAIN):
+            stage[:, k * ROWS_CHAIN + i, :] = bias[:, i * width : (i + 1) * width]
+
+    chains = ROWS_STEP // ROWS_CHAIN
+    held = {}
+    for turn in range(chains + 3):
+        if 0 <= turn - 3:
+            fourth(turn - 3, held.pop((2, turn - 3)))
+        if 0 <= turn - 2 < chains:
+            held[2, turn - 2] = third(held.pop((1, turn - 2)))
+        if 0 <= turn - 1 < chains:
+            held[1, turn - 1] = second(held.pop((0, turn - 1)))
+        if turn < chains:
+            held[0, turn] = first(turn)
+
+    rows = pl.ds(pl.multiple_of(step * ROWS_STEP, ROWS_STEP), ROWS_STEP)
+    send[:, rows, :] = stage[...].astype(jnp.bfloat16)
+    for k in range(1, peers):
+        to = other(k)
+        pltpu.make_async_remote_copy(
+            src_ref=send.at[pl.ds(to * group, group), rows, :],
+            dst_ref=out_ref.at[col, :, rows, :],
+            send_sem=send_sem.at[k - 1],
+            recv_sem=recv_sem.at[k - 1],
+            device_id=(row, to),
+            device_id_type=pl.DeviceIdType.MESH,
+        ).start()
+
+    @pl.when(step == steps - 1)
+    def _():
+        own = pltpu.make_async_copy(
+            send.at[pl.ds(col * group, group)], out_ref.at[col], own_sem
+        )
+        own.start()
+        for k in range(1, peers):
+            to = other(k)
+            done = pltpu.make_async_remote_copy(
+                src_ref=send.at[pl.ds(to * group, group)],
+                dst_ref=out_ref.at[lax.rem(col + peers - k, peers)],
+                send_sem=send_sem.at[k - 1],
+                recv_sem=recv_sem.at[k - 1],
+                device_id=(row, to),
+                device_id_type=pl.DeviceIdType.MESH,
+            )
+            done.wait()
+        own.wait()
+
+
+def pair_bias_rows(pair, trans_in, trans_out, bias_w):
+    rows, cols, _ = pair.shape
+    peers = lax.axis_size("col")
+    heads = bias_w.shape[1]
+    hidden = trans_in.shape[2]
+    eye = jnp.eye(CZ, dtype=jnp.float32) - 1.0 / CZ
+    centre = jnp.concatenate([eye, jnp.full((16, CZ), 1.0 / CZ, jnp.float32)]).astype(jnp.bfloat16)
+    halved = trans_in * jnp.array([0.5, 1.0], jnp.bfloat16)[None, :, None]
+    win = halved.reshape(CZ, 2 * hidden).T
+    whole = lambda *shape: pl.BlockSpec(shape, lambda i: (0,) * len(shape))
+    return pl.pallas_call(
+        functools.partial(pair_kernel, peers),
+        grid=(rows // ROWS_STEP,),
+        out_shape=jax.ShapeDtypeStruct((peers, heads // peers, rows, cols), jnp.bfloat16),
+        in_specs=[
+            pl.BlockSpec((ROWS_STEP, cols, CZ), lambda i: (i, 0, 0)),
+            whole(CZ + 16, CZ),
+            whole(2 * hidden, CZ),
+            whole(CZ, hidden),
+            whole(heads, CZ),
+        ],
+        out_specs=pl.BlockSpec(memory_space=pl.ANY),
+        scratch_shapes=[
+            pltpu.VMEM((heads, ROWS_STEP, cols), jnp.float32),
+            pltpu.VMEM((heads, rows, cols), jnp.bfloat16),
+            pltpu.SemaphoreType.DMA((peers - 1,)),
+            pltpu.SemaphoreType.DMA((peers - 1,)),
+            pltpu.SemaphoreType.DMA,
+        ],
+        compiler_params=pltpu.CompilerParams(
+            collective_id=0, has_side_effects=True, vmem_limit_bytes=40 * 2**20,
+            dimension_semantics=("arbitrary",),
+        ),
+        cost_estimate=pl.CostEstimate(
+            flops=2 * rows * cols * CZ * (3 * hidden + heads + CZ),
+            bytes_accessed=2 * rows * cols * (CZ + 2 * heads),
+            transcendentals=rows * cols * hidden,
+        ),
+        name="pair_bias",
+    )(pair, centre, win, trans_out.T, bias_w.T)
 
 
 def body(
@@ -126,57 +262,58 @@
     )
     query_rows = single.shape[0]
     row_start = lax.axis_index("row") * query_rows
-    within = atom_token - row_start
-    onehot = (jnp.arange(query_rows)[:, None] == within[None, :]).astype(jnp.bfloat16)
-    features = jax.nn.relu(jnp.dot(atoms_mid, agg_w, preferred_element_type=jnp.float32)).astype(
+    row_atoms = lax.all_gather(atoms_mid, "col", axis=0, tiled=True)
+    row_tokens = lax.all_gather(atom_token, "col", axis=0, tiled=True)
+    wo_full = lax.all_gather(token_wo, "col", axis=0, tiled=True)
+    back_full = lax.all_gather(back_w, "col", axis=0, tiled=True)
+    bias_rows = pair_bias_rows(pair, trans_in, trans_out, bias_w)
+    slots = jnp.arange(query_rows)
+    onehot = (slots[:, None] == (row_tokens - row_start)[None, :]).astype(jnp.bfloat16)
+    features = jax.nn.relu(jnp.dot(row_atoms, agg_w, preferred_element_type=jnp.float32)).astype(
         jnp.bfloat16
     )
-    token_part = jnp.dot(onehot, features, preferred_element_type=jnp.float32)
-    count_part = jnp.sum(onehot.astype(jnp.float32), axis=1)
-    token_sum, token_count = (
-        lax.psum(token_part.astype(jnp.bfloat16), "col").astype(jnp.float32),
-        lax.psum(count_part.astype(jnp.bfloat16), "col").astype(jnp.float32),
-    )
+    token_sum = jnp.dot(onehot, features, preferred_element_type=jnp.float32)
+    token_count = jnp.sum(onehot.astype(jnp.float32), axis=1)
     token_in = rounded(single.astype(jnp.float32) + token_sum / token_count[:, None])
-    key_cols = pair.shape[1]
-    blocks = pair.reshape(query_rows // 16, 16, key_cols, pair.shape[2])
-    bias_blocks = lax.map(lambda tile: pair_block(tile, trans_in, trans_out, bias_w), blocks)
-    pair_bias = jnp.moveaxis(bias_blocks, 1, 0).reshape(HEADS, query_rows, key_cols)
     token_norm = layer_norm(token_in.astype(jnp.float32)).astype(jnp.bfloat16)
-    token_proj = jnp.einsum(
-        "td,dme->tme", token_norm, token_w, preferred_element_type=jnp.float32
-    ).astype(jnp.bfloat16)
     head_cols = token_w.shape[2]
+    token_proj = (
+        jnp.dot(
+            token_norm, token_w.reshape(token_w.shape[0], 4 * head_cols),
+            preferred_element_type=jnp.float32,
+        )
+        .astype(jnp.bfloat16)
+        .reshape(query_rows, 4, head_cols)
+    )
     kv_rows = lax.all_gather(token_proj[:, 1:3, :], "row", axis=0, tiled=True)
     all_tokens = kv_rows.shape[0]
-    bias_rows = lax.all_to_all(pair_bias, "col", split_axis=0, concat_axis=2, tiled=True)
     heads_here = head_cols // HEAD
     query_part = token_proj[:, 0, :].reshape(query_rows, heads_here, HEAD)
     token_keys = kv_rows[:, 0, :].reshape(all_tokens, heads_here, HEAD)
     token_values = kv_rows[:, 1, :].reshape(all_tokens, heads_here, HEAD)
+    token_bias = bias_rows.transpose(1, 2, 0, 3).reshape(heads_here, query_rows, all_tokens)
     token_scores = jnp.einsum(
         "ihe,jhe->hij", query_part, token_keys, preferred_element_type=jnp.float32
     ) / math.sqrt(HEAD)
-    token_weights = softmax_rows(token_scores + bias_rows.astype(jnp.float32))
+    token_weights = softmax_rows(token_scores + token_bias.astype(jnp.float32))
     token_attn = jnp.einsum(
         "hij,jhe->ihe", token_weights, token_values, preferred_element_type=jnp.float32
     ).reshape(query_rows, head_cols)
     token_gated = (jax.nn.sigmoid(token_proj[:, 3, :].astype(jnp.float32)) * token_attn).astype(
         jnp.bfloat16
     )
+    gated_full = lax.all_gather(token_gated, "col", axis=1, tiled=True)
+    single_full = (
+        token_in.astype(jnp.float32)
+        + jnp.dot(gated_full, wo_full, preferred_element_type=jnp.float32)
+    ).astype(jnp.bfloat16)
     own_cols = token_wo.shape[0]
-    own_input = lax.dynamic_slice_in_dim(token_in, lax.axis_index("col") * own_cols, own_cols, 1)
-    projection = lax.psum_scatter(
-        jnp.dot(token_gated, token_wo, preferred_element_type=jnp.float32).astype(jnp.bfloat16),
-        "col",
-        scatter_dimension=1,
-        tiled=True,
-    ).astype(jnp.float32)
-    single_out = (own_input.astype(jnp.float32) + projection).astype(jnp.bfloat16)
-    back_sum = lax.psum(
-        jnp.dot(single_out, back_w, preferred_element_type=jnp.float32).astype(jnp.bfloat16), "col"
-    )
-    picked = jnp.einsum("ta,tc->ac", onehot, back_sum, preferred_element_type=jnp.float32)
+    single_out = lax.dynamic_slice_in_dim(
+        single_full, lax.axis_index("col") * own_cols, own_cols, 1
+    )
+    back = jnp.dot(single_full, back_full, preferred_element_type=jnp.float32).astype(jnp.bfloat16)
+    own_hot = (slots[None, :] == (atom_token - row_start)[:, None]).astype(jnp.bfloat16)
+    picked = jnp.dot(own_hot, back, preferred_element_type=jnp.float32)
     atoms_out = (atoms_mid.astype(jnp.float32) + picked).astype(jnp.bfloat16)
     return (single_out, atoms_out)
 

time: 366 us -> 239 us (0.65)
  waiting for transfers between devices: 130 us -> 0.02 us
  blocking collectives: 40 us -> 123 us
  matrix products: 86.9 us -> 15.2 us
  other arithmetic: 68.5 us -> 5.48 us
  Pallas kernels: 0 us -> 53.7 us
  local copies, waits for them, and re-layouts: 8.57 us -> 19.4 us
  starting transfers between devices: 13.2 us -> 6.79 us
    all_gather x0 -> x4, blocking collectives: none -> 117 us  [the longest x1 31.3 us: body(): gated_full = lax.all_gather(token_gated, 'col', axis=1, tiled=True)]
    dot_general x52 -> x4, matrix products: 78.9 us -> 5.98 us  [the longest x1 2.06 us: body(): token_sum = jnp.dot(onehot, features, preferred_element_type=jnp.float32)]
    psum x2 -> x0, waiting for transfers between devices: 68.8 us -> none  [the longest x1 68.8 us: body(): lax.psum(jnp.dot(single_out, back_w, preferred_element_type=jnp.float32)....]
    unnamed x4 -> x1, waiting for transfers between devices: 61.5 us -> 0.02 us
    pallas_call x0 -> x1, Pallas kernels: none -> 53.7 us  [pair_bias_rows(): pl.pallas_call(functools.partial(pair_kernel, peers), grid=(rows // ROWS_...]
    reduce_sum x35 -> x3, other arithmetic: 39 us -> 1.36 us  [layer_norm(): spread = jnp.mean(centred * centred, axis=-1, keepdims=True)]
    psum x1 -> x0, blocking collectives: 33.9 us -> none  [body(): lax.psum(count_part.astype(jnp.bfloat16), 'col').astype(jnp.float32)]
    reduce_sum x35 -> x3, other arithmetic: 25.3 us -> 1.09 us  [layer_norm(): centred = values - jnp.mean(values, axis=-1, keepdims=True)]
  transfers between devices with their start and end apart: 6 -> 3, of which waited for: 2 -> 0; matrix products, arithmetic and copies ran while one was open for 40% -> 12% of each run, Pallas kernels for 0% -> 23%
where the time goes in v1:
time: 239 us; the launch traced here: 238 us
  blocking collectives  123 us (51%)
  Pallas kernels  53.7 us (22%)
  local copies, waits for them, and re-layouts  19.4 us (8%)
  matrix products  15.2 us (6%)
  between operations  14.5 us (6%)
  starting transfers between devices  6.79 us (3%)
  other arithmetic  5.48 us (2%)
    pallas_call x1, Pallas kernels, pair_bias_rows(): pl.pallas_call(functools.partial(pair_kernel, peers), grid=(rows // ROWS_...  53.7 us
    all_gather x1, blocking collectives, body(): gated_full = lax.all_gather(token_gated, 'col', axis=1, tiled=True)  31.3 us
    all_gather x1, blocking collectives, body(): row_atoms = lax.all_gather(atoms_mid, 'col', axis=0, tiled=True)  31 us
    all_gather x1, blocking collectives, body(): back_full = lax.all_gather(back_w, 'col', axis=0, tiled=True)  30.8 us
    all_gather x1, blocking collectives, body(): row_tokens = lax.all_gather(atom_token, 'col', axis=0, tiled=True)  23.8 us
    unnamed x31, local copies, waits for them, and re-layouts  9.1 us
    all_gather x1, blocking collectives, body(): kv_rows = lax.all_gather(token_proj[:, 1:3, :], 'row', axis=0, tiled=True)  6.35 us
    ppermute x1, starting transfers between devices, extended_2(): before = lax.ppermute(last, axis, up)  5.47 us
  transfers between devices with their start and end apart: 3, of which 0 were waited for; matrix products, arithmetic and copies ran while one was open for 12% of the time, Pallas kernels for 23%

profile of v1, /device:TPU:0, one launch (start us, length us, event | category | flops | bytes accessed | tf_op | source)
XLA Modules:
  0.0 238.2 jit_solution(14586351960032284712)
XLA Ops:
  8.0 1.3 collective-permute-start.1
  9.3 5.5 %collective-permute-start = (bf16[48,128]{1,0:T(8,128)(2,1)S(1)}, bf16[48,128]{1,0:T(8,128)(2,1)S(1)}, u32[]{:S(2)}, u32[]{:S(2)}) collective-permute-start(bf16[48,128]{1,0:T(8,128)(2,1)S(1)} %get-tuple-element.18), channel_id=1, source_target_pairs={{0,1},{1,2},{2,3},{3,4},{4,5},{5,6},{6,7},{7,8},{8,9},{9,10},{10,1... | collective-permute-start | bytes 36872 | tf_op jit(solution)/shard_map/ppermute | solution.py:32
  15.7 0.9 fusion.34
  16.7 23.8 %all-gather = s32[8,1,128]{2,1,0:T(1,128)S(1)} all-gather(s32[1,1,128]{2,1,0:T(1,128)} %bitcast.98), channel_id=1, replica_groups=mesh['row'=4,'col'=8] {'col'}, dimensions={0}, use_global_device_ids=true | all-gather | bytes 4608 | tf_op jit(solution)/shard_map/all_gather | solution.py:266
  41.4 1.1 broadcast_multiply_fusion
  42.6 0.9 copy.71
  43.6 3.5 %copy-done.1 = bf16[256,128,128]{2,1,0:T(8,128)(2,1)S(1)} copy-done((bf16[256,128,128]{2,1,0:T(8,128)(2,1)S(1)}, bf16[256,128,128]{2,1,0:T(8,128)(2,1)}, u32[]{:S(2)}) %copy-start.1) | copy-done | bytes 8388632
  47.8 53.7 %pair_bias.1 = bf16[8,2,256,128]{3,2,1,0:T(8,128)(2,1)S(1)} custom-call(bf16[256,128,128]{2,1,0:T(8,128)(2,1)S(1)} %copy-done.1, bf16[144,128]{1,0:T(8,128)(2,1)S(1)} %concatenate.7.centre_ref, bf16[512,128]{1,0:T(8,128)(2,1)S(1)} %bitcast.83, bf16[128,256]{1,0:T(8,128)(2,1)S(1)} %bitcast.84, bf16[16,128]{1,0:T(8,128)(2,1)S(1)} %bitcast.85), custom_call_target="tpu_custom_call" | custom-call | flops 7650410496 | bytes 10485760 | tf_op jit(solution)/shard_map/pair_bias/pallas_call | solution.py:166
  103.1 30.8 %all_gather.23 = bf16[768,128]{1,0:T(8,128)(2,1)S(1)} all-gather(bf16[96,128]{1,0:T(8,128)(2,1)S(1)} %copy-done.11), channel_id=1, replica_groups=mesh['row'=4,'col'=8] {'col'}, dimensions={0}, use_global_device_ids=true | all-gather | bytes 221184 | tf_op jit(solution)/shard_map/all_gather | solution.py:268
  134.7 1.9 copy.72
  136.6 1.9 copy.73
  140.8 1.1 fusion.9
  142.2 2.6 %convolution_bitcast_fusion = f32[4,32,4,32]{1,3,2,0:T(8,128)} fusion(bf16[4,128,4,32]{1,3,2,0:T(8,128)(2,1)} %bitcast.94, f32[4,4,32]{2,1,0:T(4,128)S(1)} %fusion.59, f32[4,4,32,128]{3,2,1,0:T(8,128)S(1)} %fusion.9), kind=kOutput, calls=%fused_computation.21 | convolution fusion | flops 4391551 | bytes 460800 | tf_op jit(solution)/shard_map/whij,wjha->wiha/dot_general | solution.py:256
  144.7 1.1 copy.68
  147.5 31.0 %all_gather.19 = bf16[1024,128]{1,0:T(8,128)(2,1)S(1)} all-gather(bf16[128,128]{1,0:T(8,128)(2,1)S(1)} %fusion.11), channel_id=1, replica_groups=mesh['row'=4,'col'=8] {'col'}, dimensions={0}, use_global_device_ids=true | all-gather | bytes 294912 | tf_op jit(solution)/shard_map/all_gather | solution.py:265
  178.5 2.1 fusion.6
  181.0 1.1 convolution_convert_fusion
  182.1 1.1 copy.69
  183.2 6.4 %all_gather.20 = bf16[1024,2,96]{0,2,1:T(8,128)(2,1)S(1)} all-gather(bf16[256,2,96]{0,2,1:T(8,128)(2,1)S(1)} %slice.90), channel_id=1, replica_groups=mesh['row'=4,'col'=8] {'row'}, dimensions={0}, use_global_device_ids=true | all-gather | bytes 491520 | tf_op jit(solution)/shard_map/all_gather | solution.py:288
  190.7 1.3 copy-done.3
  193.0 3.4 %fusion.14 = f32[2,48,256]{2,1,0:T(8,128)S(1)} fusion(bf16[1024,2,48]{0,2,1:T(8,128)(2,1)S(1)} %bitcast.93, f32[2,256]{1,0:T(2,128)S(1)} %fusion.60, f32[2,256,1024]{2,1,0:T(8,128)} %copy-done.3), kind=kOutput, calls=%fused_computation.32 | convolution fusion | flops 51906048 | bytes 2394112 | tf_op jit(solution)/shard_map/hij,jhe->ihe/dot_general | solution.py:299
  196.5 31.3 %all_gather.21 = bf16[256,768]{0,1:T(8,128)(2,1)S(1)} all-gather(bf16[256,96]{0,1:T(8,128)(2,1)S(1)} %fusion.31), channel_id=1, replica_groups=mesh['row'=4,'col'=8] {'col'}, dimensions={1}, use_global_device_ids=true | all-gather | bytes 442368 | tf_op jit(solution)/shard_map/all_gather | solution.py:305
  227.7 1.8 fusion.5
  230.3 1.0 fusion.12
  (75 shorter events, 13.3 us)
Async XLA Ops:
  7.2 173.8 %copy-start = (bf16[768,4,96]{0,2,1:T(8,128)(2,1)S(1)}, bf16[768,4,96]{0,2,1:T(8,128)(2,1)}, u32[]{:S(2)}) copy-start(bf16[768,4,96]{0,2,1:T(8,128)(2,1)} %param.28) | copy-start | bytes 1769476
  7.2 220.5 %all-gather.3.cloned.1.call-start = ((), (), s32[]{:S(2)}) async-start(), calls=%async_computation | async-start | bytes 1327104 | tf_op jit(solution)/shard_map/all_gather | solution.py:267
  8.0 130.5 %collective-permute-start.1 = (bf16[48,128]{1,0:T(8,128)(2,1)S(1)}, bf16[48,128]{1,0:T(8,128)(2,1)S(1)}, u32[]{:S(2)}, u32[]{:S(2)}) collective-permute-start(bf16[48,128]{1,0:T(8,128)(2,1)S(1)} %get-tuple-element.19), channel_id=1, source_target_pairs={{1,0},{2,1},{3,2},{4,3},{5,4},{6,5},{7,6},{8,7},{9,8},{10,9},{11,1... | collective-permute-start | bytes 36872 | tf_op jit(solution)/shard_map/ppermute | solution.py:33
  9.3 129.2 %collective-permute-start = (bf16[48,128]{1,0:T(8,128)(2,1)S(1)}, bf16[48,128]{1,0:T(8,128)(2,1)S(1)}, u32[]{:S(2)}, u32[]{:S(2)}) collective-permute-start(bf16[48,128]{1,0:T(8,128)(2,1)S(1)} %get-tuple-element.18), channel_id=1, source_target_pairs={{0,1},{1,2},{2,3},{3,4},{4,5},{5,6},{6,7},{7,8},{8,9},{9,10},{10,1... | collective-permute-start | bytes 36872 | tf_op jit(solution)/shard_map/ppermute | solution.py:32
  43.6 3.5 %copy-start.1 = (bf16[256,128,128]{2,1,0:T(8,128)(2,1)S(1)}, bf16[256,128,128]{2,1,0:T(8,128)(2,1)}, u32[]{:S(2)}) copy-start(bf16[256,128,128]{2,1,0:T(8,128)(2,1)} %pair_ref.1) | copy-start | bytes 25165828
  47.1 0.7 copy-start.2
  101.5 1.0 copy-start.5
  101.5 1.0 copy-start.12
  101.5 1.3 copy-start.4
  101.6 1.3 copy-start.6
  101.6 1.5 copy-start.11
  103.1 30.8 %copy-start.7 = (bf16[128,4,128]{2,0,1:T(8,128)(2,1)}, bf16[128,4,128]{2,0,1:T(8,128)(2,1)S(1)}, u32[]{:S(2)}) copy-start(bf16[128,4,128]{2,0,1:T(8,128)(2,1)S(1)} %convolution_convert_fusion.1) | copy-start | bytes 393220
  139.2 6.8 %copy-start.13 = (bf16[128,128]{1,0:T(8,128)(2,1)S(1)}, bf16[128,128]{1,0:T(8,128)(2,1)}, u32[]{:S(2)}) copy-start(bf16[128,128]{1,0:T(8,128)(2,1)} %param.23) | copy-start | bytes 98308
  146.9 0.6 copy-start.9
  190.7 1.4 copy-start.3
  192.0 0.9 copy-start.8
  196.4 34.0 %copy-start.10 = (bf16[128,128]{1,0:T(8,128)(2,1)S(1)}, bf16[128,128]{1,0:T(8,128)(2,1)}, u32[]{:S(2)}) copy-start(bf16[128,128]{1,0:T(8,128)(2,1)} %copy-done.9) | copy-start | bytes 98308
Sparse Core Ops, SparseCore 0:
  14.9 48.3 all-gather.2

commit v2 on v1

v2 whole, which is shorter than its diff:
```python
import functools
import math

import jax
import jax.numpy as jnp
from jax import lax
from jax.experimental import pallas as pl
from jax.experimental.pallas import tpu as pltpu
from jax.sharding import PartitionSpec as P

HEADS = 16
HEAD = 48
CA = 128
CZ = 128
ATOM_HEADS = 4
ATOM_HEAD = 32
QW = 32
KW = 128
RIM = (KW - QW) // 2
LANES = 128
ROWS_STEP = 16
ROWS_CHAIN = 2
ATOM_STEP = 1
TOKEN_STEP = 4
MESH = pl.DeviceIdType.MESH


epsilon = 1e-05
masked_score = -1e30


def layer_norm(values):
    centred = values - jnp.mean(values, axis=-1, keepdims=True)
    spread = jnp.mean(centred * centred, axis=-1, keepdims=True)
    return centred * lax.rsqrt(spread + epsilon)


def softmax_rows(scores):
    highest = jnp.max(scores, axis=-1, keepdims=True)
    raised = jnp.exp(scores - highest)
    return (raised / jnp.sum(raised, axis=-1, keepdims=True)).astype(jnp.bfloat16)


def dot(a, b):
    return jnp.dot(a, b, preferred_element_type=jnp.float32)


def dot_rows(a, b):
    return lax.dot_general(a, b, (((1,), (1,)), ((), ())), preferred_element_type=jnp.float32)


def whole_kernel(
    peers, rows_n,
    pair_ref, centre_ref, win_ref, wout_ref, bw_ref,
    atoms_ref, atom_pair_ref, token_ref, single_ref, atom_w_ref, pair_w_ref, atom_wo_ref,
    agg_ref, token_w_ref, wo_ref, back_ref,
    single_out_ref, atoms_out_ref,
    stage, send, bias_all, before, after, mid_all, token_all, hot, token_in, proj, kv_all,
    part_send, part_all, pick_send, pick_all,
    halo_s, halo_r, tok_s, tok_r, mid_s, mid_r, kv_s, kv_r, bias_s, bias_r,
    part_s, part_r, pick_s, pick_r,
):
    step = pl.program_id(0)
    steps = pl.num_programs(0)
    row, col = lax.axis_index("row"), lax.axis_index("col")
    group = send.shape[0] // peers
    width = pair_ref.shape[1]
    atom_count = atoms_ref.shape[0]
    query_rows = single_ref.shape[0]
    own_cols = back_ref.shape[1]

    def other(k):
        return lax.rem(col + k, peers)

    def source(k):
        return lax.rem(col + peers - k, peers)

    def other_row(k):
        return lax.rem(row + k, rows_n)

    def source_row(k):
        return lax.rem(row + rows_n - k, rows_n)

    def to_col(k, src, dst, s, r):
        return pltpu.make_async_remote_copy(
            src_ref=src, dst_ref=dst, send_sem=s.at[k - 1], recv_sem=r.at[k - 1],
            device_id=(row, other(k)), device_id_type=MESH,
        )

    def to_row(k, src, dst):
        return pltpu.make_async_remote_copy(
            src_ref=src, dst_ref=dst, send_sem=kv_s.at[k - 1], recv_sem=kv_r.at[k - 1],
            device_id=(other_row(k), col), device_id_type=MESH,
        )

    is_first = jnp.logical_and(row == 0, col == 0)
    is_last = jnp.logical_and(row == rows_n - 1, col == peers - 1)
    wraps_up = jnp.logical_and(col == peers - 1, row < rows_n - 1)
    wraps_down = jnp.logical_and(col == 0, row > 0)
    up = (lax.rem(jnp.where(col == peers - 1, row + 1, row), rows_n), lax.rem(col + 1, peers))
    down = (
        lax.rem(jnp.where(col == 0, row + rows_n - 1, row), rows_n),
        lax.rem(col + peers - 1, peers),
    )

    def halo_up():
        return pltpu.make_async_remote_copy(
            src_ref=atoms_ref.at[pl.ds(atom_count - RIM, RIM)], dst_ref=before,
            send_sem=halo_s.at[0], recv_sem=halo_r.at[0], device_id=up, device_id_type=MESH,
        )

    def halo_down():
        return pltpu.make_async_remote_copy(
            src_ref=atoms_ref.at[pl.ds(0, RIM)], dst_ref=after,
            send_sem=halo_s.at[1], recv_sem=halo_r.at[1], device_id=down, device_id_type=MESH,
        )

    @pl.when(step == 0)
    def _():
        barrier = pltpu.get_barrier_semaphore()
        for k in range(1, peers):
            pl.semaphore_signal(barrier, inc=1, device_id=(row, other(k)), device_id_type=MESH)
        for k in range(1, rows_n):
            pl.semaphore_signal(barrier, inc=1, device_id=(other_row(k), col), device_id_type=MESH)

        @pl.when(wraps_up)
        def _():
            pl.semaphore_signal(barrier, inc=1, device_id=up, device_id_type=MESH)

        @pl.when(wraps_down)
        def _():
            pl.semaphore_signal(barrier, inc=1, device_id=down, device_id_type=MESH)

        extra = wraps_up.astype(jnp.int32) + wraps_down.astype(jnp.int32)
        pl.semaphore_wait(barrier, peers + rows_n - 2 + extra)

        @pl.when(jnp.logical_not(is_last))
        def _():
            halo_up().start()

        @pl.when(jnp.logical_not(is_first))
        def _():
            halo_down().start()

        @pl.when(is_first)
        def _():
            before[...] = jnp.zeros_like(before)

        @pl.when(is_last)
        def _():
            after[...] = jnp.zeros_like(after)

        token_all[col] = token_ref[...]
        for k in range(1, peers):
            to_col(k, token_ref, token_all.at[col], tok_s, tok_r).start()

    @pl.when(step == ATOM_STEP)
    def _():
        @pl.when(jnp.logical_not(is_last))
        def _():
            halo_up().wait_send()
            halo_down().wait_recv()

        @pl.when(jnp.logical_not(is_first))
        def _():
            halo_down().wait_send()
            halo_up().wait_recv()

        own = atoms_ref[...].astype(jnp.float32)
        extended = jnp.concatenate(
            [before[...].astype(jnp.float32), own, after[...].astype(jnp.float32)]
        )
        projected = dot(layer_norm(extended).astype(jnp.bfloat16), atom_w_ref[...])
        projected = projected.astype(jnp.bfloat16)
        query = projected[RIM : RIM + atom_count, :CA]
        gate = projected[RIM : RIM + atom_count, 3 * CA :].astype(jnp.float32)
        lane = lax.broadcasted_iota(jnp.int32, (QW, CA), 1)
        heads = [
            jnp.logical_and(lane >= h * ATOM_HEAD, lane < (h + 1) * ATOM_HEAD)
            for h in range(ATOM_HEADS)
        ]
        start = (row * peers + col) * atom_count - RIM
        all_atoms = atom_count * peers * rows_n
        spot = lax.broadcasted_iota(jnp.int32, (ATOM_HEADS * QW, KW), 1)
        attended = []
        for window in range(atom_count // QW):
            low = window * QW
            queries = query[low : low + QW].astype(jnp.float32)
            stacked = jnp.concatenate(
                [jnp.where(mask, queries, 0.0) for mask in heads]
            ).astype(jnp.bfloat16)
            planes = [
                atom_pair_ref[window, c].astype(jnp.float32)
                for c in range(atom_pair_ref.shape[1])
            ]
            bias = []
            for h in range(ATOM_HEADS):
                total = planes[0] * pair_w_ref[0, h]
                for c in range(1, len(planes)):
                    total = total + planes[c] * pair_w_ref[c, h]
                bias.append(total)
            scores = dot_rows(stacked, projected[low : low + KW, CA : 2 * CA])
            scores = scores / math.sqrt(ATOM_HEAD) + jnp.concatenate(bias)
            place = spot + (start + low)
            inside = jnp.logical_and(place >= 0, place < all_atoms)
            weights = softmax_rows(jnp.where(inside, scores, masked_score))
            mixed = dot(weights, projected[low : low + KW, 2 * CA : 3 * CA])
            picked = jnp.where(heads[0], mixed[:QW], 0.0)
            for h in range(1, ATOM_HEADS):
                picked = picked + jnp.where(heads[h], mixed[h * QW : (h + 1) * QW], 0.0)
            attended.append(picked)
        gated = (jax.nn.sigmoid(gate) * jnp.concatenate(attended)).astype(jnp.bfloat16)
        mid_all[col] = (own + dot(gated, atom_wo_ref[...])).astype(jnp.bfloat16)
        for k in range(1, peers):
            to_col(k, mid_all.at[col], mid_all.at[col], mid_s, mid_r).start()

    @pl.when(step == TOKEN_STEP)
    def _():
        for k in range(1, peers):
            to_col(k, token_ref, token_all.at[source(k)], tok_s, tok_r).wait()
            to_col(k, mid_all.at[col], mid_all.at[source(k)], mid_s, mid_r).wait()
        slots = lax.broadcasted_iota(jnp.int32, (query_rows, LANES), 0) + row * query_rows
        counts = jnp.zeros((query_rows, LANES), jnp.float32)
        for c in range(peers):
            match = (slots == token_all[c][0:1, :]).astype(jnp.float32)
            counts = counts + match
            hot[:, c * LANES : (c + 1) * LANES] = match.astype(jnp.bfloat16)
        count = jnp.sum(counts, axis=1, keepdims=True)
        mids = mid_all[...].reshape(peers * atom_count, CA)
        features = jnp.maximum(dot(mids, agg_ref[...]), 0.0).astype(jnp.bfloat16)
        sums = dot(hot[...], features)
        held = (single_ref[...].astype(jnp.float32) + sums / count).astype(jnp.bfloat16)
        token_in[...] = held
        normed = layer_norm(held.astype(jnp.float32)).astype(jnp.bfloat16)
        proj[...] = dot(normed, token_w_ref[...]).astype(jnp.bfloat16)
        kv_all[row] = proj[:, LANES : 3 * LANES]
        for k in range(1, rows_n):
            to_row(k, kv_all.at[row], kv_all.at[row]).start()

    def first(k):
        x = pair_ref[k * ROWS_CHAIN : (k + 1) * ROWS_CHAIN].reshape(ROWS_CHAIN * width, CZ)
        both = dot_rows(centre_ref[...], x)
        centred = both[:CZ]
        spread = jnp.mean(centred * centred, axis=0, keepdims=True)
        normed = (centred * lax.rsqrt(spread + epsilon)).astype(jnp.bfloat16)
        return centred, both[CZ : CZ + 1], normed

    def second(state):
        centred, average, normed = state
        both = dot(win_ref[...], normed)
        half = both.shape[0] // 2
        gate = both[:half]
        hidden = ((gate + gate * jnp.tanh(gate)) * both[half:]).astype(jnp.bfloat16)
        return centred + average, hidden

    def third(state):
        tile, hidden = state
        update = dot(wout_ref[...], hidden)
        renewed = (tile + update).astype(jnp.bfloat16).astype(jnp.float32)
        centred = renewed - jnp.mean(renewed, axis=0, keepdims=True)
        spread = jnp.mean(centred * centred, axis=0, keepdims=True)
        return (centred * lax.rsqrt(spread + epsilon)).astype(jnp.bfloat16)

    def fourth(k, renormed):
        bias = dot(bw_ref[...], renormed)
        for i in range(ROWS_CHAIN):
            stage[:, k * ROWS_CHAIN + i, :] = bias[:, i * width : (i + 1) * width]

    chains = ROWS_STEP // ROWS_CHAIN
    held = {}
    for turn in range(chains + 3):
        if 0 <= turn - 3:
            fourth(turn - 3, held.pop((2, turn - 3)))
        if 0 <= turn - 2 < chains:
            held[2, turn - 2] = third(held.pop((1, turn - 2)))
        if 0 <= turn - 1 < chains:
            held[1, turn - 1] = second(held.pop((0, turn - 1)))
        if turn < chains:
            held[0, turn] = first(turn)

    rows = pl.ds(pl.multiple_of(step * ROWS_STEP, ROWS_STEP), ROWS_STEP)
    send[:, rows, :] = stage[...].astype(jnp.bfloat16)
    bias_all[col, :, rows, :] = send[pl.ds(col * group, group), rows, :]
    for k in range(1, peers):
        to_col(
            k, send.at[pl.ds(other(k) * group, group), rows, :], bias_all.at[col, :, rows, :],
            bias_s, bias_r,
        ).start()

    @pl.when(step == steps - 1)
    def _():
        for k in range(1, rows_n):
            to_row(k, kv_all.at[row], kv_all.at[source_row(k)]).wait()
        for k in range(1, peers):
            to_col(
                k, send.at[pl.ds(other(k) * group, group)], bias_all.at[source(k)], bias_s, bias_r
            ).wait()
        query = proj[:, :LANES].astype(jnp.float32)
        keys = kv_all[:, :, :LANES].reshape(rows_n * query_rows, LANES)
        values = kv_all[:, :, LANES:].reshape(rows_n * query_rows, LANES)
        lane = lax.broadcasted_iota(jnp.int32, (query_rows, LANES), 1)
        attended = jnp.zeros((query_rows, LANES), jnp.float32)
        for h in range(group):
            mask = jnp.logical_and(lane >= h * HEAD, lane < (h + 1) * HEAD)
            scores = dot_rows(jnp.where(mask, query, 0.0).astype(jnp.bfloat16), keys)
            bias = jnp.concatenate([bias_all[c, h] for c in range(peers)], axis=1)
            weights = softmax_rows(scores / math.sqrt(HEAD) + bias.astype(jnp.float32))
            attended = attended + jnp.where(mask, dot(weights, values), 0.0)
        gate = proj[:, 3 * LANES :].astype(jnp.float32)
        gated = (jax.nn.sigmoid(gate) * attended).astype(jnp.bfloat16)
        part = dot_rows(wo_ref[...], gated).astype(jnp.bfloat16)
        part_send[...] = part.reshape(peers, own_cols, query_rows)
        for k in range(1, peers):
            to_col(k, part_send.at[other(k)], part_all.at[col], part_s, part_r).start()
        spot = lax.broadcasted_iota(jnp.int32, (own_cols, token_in.shape[1]), 0) + col * own_cols
        column = lax.broadcasted_iota(jnp.int32, (own_cols, token_in.shape[1]), 1)
        chosen = (spot == column).astype(jnp.float32).astype(jnp.bfloat16)
        total = dot_rows(chosen, token_in[...])
        part_all[col] = part_send[col]
        for k in range(1, peers):
            to_col(k, part_send.at[other(k)], part_all.at[source(k)], part_s, part_r).wait()
        update = part_all[0].astype(jnp.float32)
        for c in range(1, peers):
            update = update + part_all[c].astype(jnp.float32)
        fresh = total + update
        single_t = fresh.astype(jnp.bfloat16)
        back = dot(back_ref[...], single_t).astype(jnp.bfloat16)
        picks = dot(back, hot[...]).astype(jnp.bfloat16)
        for c in range(peers):
            pick_send[c] = picks[:, c * LANES : (c + 1) * LANES]
        for k in range(1, peers):
            to_col(k, pick_send.at[other(k)], pick_all.at[col], pick_s, pick_r).start()
        rest = LANES - own_cols
        padded = jnp.concatenate([fresh, jnp.zeros((rest, query_rows), jnp.float32)])
        single_out_ref[...] = padded.T[:, :own_cols].astype(jnp.bfloat16)
        pick_all[col] = pick_send[col]
        for k in range(1, peers):
            to_col(k, pick_send.at[other(k)], pick_all.at[source(k)], pick_s, pick_r).wait()
        total_back = pick_all[0].astype(jnp.float32)
        for c in range(1, peers):
            total_back = total_back + pick_all[c].astype(jnp.float32)
        total_back = total_back.astype(jnp.bfloat16).astype(jnp.float32).T
        atoms_out_ref[...] = (mid_all[col].astype(jnp.float32) + total_back).astype(jnp.bfloat16)


def body(
    atoms, atom_pair, atom_token, single, pair, atom_w, atom_pair_w, atom_wo, agg_w, trans_in,
    trans_out, bias_w, token_w, token_wo, back_w,
):
    rows, cols, _ = pair.shape
    peers, rows_n = lax.axis_size("col"), lax.axis_size("row")
    heads = bias_w.shape[1]
    hidden = trans_in.shape[2]
    atom_count = atoms.shape[0]
    width = single.shape[1]
    own_cols = token_wo.shape[0]
    bf16 = jnp.bfloat16
    eye = jnp.eye(CZ, dtype=jnp.float32) - 1.0 / CZ
    centre = jnp.concatenate([eye, jnp.full((16, CZ), 1.0 / CZ, jnp.float32)]).astype(bf16)
    halved = trans_in * jnp.array([0.5, 1.0], bf16)[None, :, None]
    win = halved.reshape(CZ, 2 * hidden).T
    rest = LANES - own_cols
    token_w_wide = jnp.pad(token_w, ((0, 0), (0, 0), (0, rest))).reshape(width, 4 * LANES)
    wo_t = jnp.pad(token_wo, ((0, rest), (0, 0))).T
    operands = (
        pair, centre, win, trans_out.T, bias_w.T,
        atoms, atom_pair, jnp.broadcast_to(atom_token[None, :], (8, atom_count)), single,
        atom_w.reshape(CA, 4 * CA), atom_pair_w.astype(jnp.float32), atom_wo, agg_w,
        token_w_wide, wo_t, back_w.T,
    )
    whole = lambda value: pl.BlockSpec(value.shape, lambda i, n=value.ndim: (0,) * n)
    in_specs = [pl.BlockSpec((ROWS_STEP, cols, CZ), lambda i: (i, 0, 0))]
    in_specs += [whole(value) for value in operands[1:]]
    in_specs[10] = pl.BlockSpec(memory_space=pltpu.SMEM)
    dma = lambda n: pltpu.SemaphoreType.DMA((n,))
    p, r = peers - 1, rows_n - 1
    return pl.pallas_call(
        functools.partial(whole_kernel, peers, rows_n),
        grid=(rows // ROWS_STEP,),
        out_shape=(
            jax.ShapeDtypeStruct((rows, own_cols), bf16),
            jax.ShapeDtypeStruct((atom_count, CA), bf16),
        ),
        in_specs=in_specs,
        out_specs=(
            pl.BlockSpec((rows, own_cols), lambda i: (0, 0)),
            pl.BlockSpec((atom_count, CA), lambda i: (0, 0)),
        ),
        scratch_shapes=[
            pltpu.VMEM((heads, ROWS_STEP, cols), jnp.float32),
            pltpu.VMEM((heads, rows, cols), bf16),
            pltpu.VMEM((peers, heads // peers, rows, cols), bf16),
            pltpu.VMEM((RIM, CA), bf16),
            pltpu.VMEM((RIM, CA), bf16),
            pltpu.VMEM((peers, atom_count, CA), bf16),
            pltpu.VMEM((peers, 8, atom_count), jnp.int32),
            pltpu.VMEM((rows, peers * atom_count), bf16),
            pltpu.VMEM((rows, width), bf16),
            pltpu.VMEM((rows, 4 * LANES), bf16),
            pltpu.VMEM((rows_n, rows, 2 * LANES), bf16),
            pltpu.VMEM((peers, own_cols, rows), bf16),
            pltpu.VMEM((peers, own_cols, rows), bf16),
            pltpu.VMEM((peers, CA, atom_count), bf16),
            pltpu.VMEM((peers, CA, atom_count), bf16),
            dma(2), dma(2), dma(p), dma(p), dma(p), dma(p), dma(r), dma(r), dma(p), dma(p),
            dma(p), dma(p), dma(p), dma(p),
        ],
        compiler_params=pltpu.CompilerParams(
            collective_id=0, has_side_effects=True, vmem_limit_bytes=56 * 2**20,
            dimension_semantics=("arbitrary",),
        ),
        cost_estimate=pl.CostEstimate(
            flops=2 * rows * cols * CZ * (3 * hidden + heads + CZ),
            bytes_accessed=2 * rows * cols * (CZ + 2 * heads),
            transcendentals=rows * cols * hidden,
        ),
        name="diffusion_block",
    )(*operands)


def solution(mesh):
    in_specs = (
        P(("row", "col"), None),
        P(("row", "col"), None, None, None),
        P(("row", "col")),
        P("row", None),
        P("row", "col", None),
        P(),
        P(),
        P(),
        P(),
        P(),
        P(),
        P(),
        P(None, None, "col"),
        P("col", None),
        P("col", None),
    )
    out_specs = (P("row", "col"), P(("row", "col"), None))
    return jax.shard_map(body, mesh=mesh, in_specs=in_specs, out_specs=out_specs, check_vma=False)
```

time: 239 us -> 102 us (0.43)
  blocking collectives: 123 us -> 0 us
  Pallas kernels: 53.7 us -> 84 us
  matrix products: 15.2 us -> 0 us
  between operations: 14.5 us -> 0.66 us
  starting transfers between devices: 6.79 us -> 0 us
  other arithmetic: 5.48 us -> 1.1 us
  local copies, waits for them, and re-layouts: 19.4 us -> 15.6 us
    all_gather x5 -> x0, blocking collectives: 123 us -> none  [the longest x1 31.3 us: body(): gated_full = lax.all_gather(token_gated, 'col', axis=1, tiled=True)]
    pallas_call x1, Pallas kernels: 53.7 us -> 84 us  [body(): pl.pallas_call(functools.partial(whole_kernel, peers, rows_n), grid=(rows...]
    dot_general x12 -> x0, matrix products: 15.2 us -> none  [the longest x1 3.42 us: body(): jnp.einsum('hij,jhe->ihe', token_weights, token_values, preferred_element...]
    ppermute x2 -> x0, starting transfers between devices: 6.75 us -> none  [the longest x1 5.47 us: extended_2(): before = lax.ppermute(last, axis, up)]
    convert_element_type x3 -> x1, local copies, waits for them, and re-layouts: 4.85 us -> 1.35 us  [body(): atom_pair_w.astype(jnp.float32)]
    slice x8 -> x0, local copies, waits for them, and re-layouts: 3.04 us -> none  [the longest x1 0.78 us: extended_2(): last = lax.slice_in_dim(value, length - width, length, axis=dim)]
    reduce_sum x7 -> x0, other arithmetic: 2.64 us -> none  [the longest x3 1.36 us: layer_norm(): spread = jnp.mean(centred * centred, axis=-1, keepdims=True)]
    unnamed x31 -> x5, local copies, waits for them, and re-layouts: 9.1 us -> 7.04 us
  transfers between devices with their start and end apart: 3 -> 0, of which waited for: 0 -> 0; matrix products, arithmetic and copies ran while one was open for 12% -> 0% of each run, Pallas kernels for 23% -> 0%
where the time goes in v2:
time: 102 us; the launch traced here: 101 us
  Pallas kernels  84 us (82%)
  local copies, waits for them, and re-layouts  15.6 us (15%)
  other arithmetic  1.1 us (1%)
    pallas_call x1, Pallas kernels, body(): pl.pallas_call(functools.partial(whole_kernel, peers, rows_n), grid=(rows...  84 us
    unnamed x5, local copies, waits for them, and re-layouts  7.04 us

profile of v2, /device:TPU:0, one launch (start us, length us, event | category | flops | bytes accessed | tf_op | source)
XLA Modules:
  0.0 101.3 jit_solution(13562539226549095049)
XLA Ops:
  0.6 1.1 %pad.10 = bf16[768,4,128]{0,2,1:T(8,128)(2,1)S(1)} pad(bf16[768,4,96]{0,2,1:T(8,128)(2,1)} %param.28, bf16[]{:T(256)} %constant.10.clone.1), padding=0_0x0_0x0_32 | pad | bytes 1376258 | tf_op jit(solution)/shard_map/jit(_pad)/pad | solution.py:363
  1.8 1.2 %copy.32.token_w_ref = bf16[768,512]{1,0:T(8,128)(2,1)} copy(bf16[768,512]{0,1:T(8,128)(2,1)S(1)} %bitcast.13) | data formatting | bytes 1572864 | tf_op jit(solution)/shard_map/reshape | solution.py:363
  2.9 1.1 %copy.28 = bf16[96,768]{0,1:T(8,128)(2,1)S(1)} copy(bf16[96,768]{1,0:T(8,128)(2,1)} %param.29) | data formatting | bytes 294912 | tf_op args[13]
  4.0 0.7 pad_bitcast_fusion.wo_ref
  4.7 1.1 %broadcast_multiply_fusion = bf16[128,2,256]{2,1,0:T(2,128)(2,1)S(1)} fusion(bf16[128,2,256]{2,1,0:T(2,128)(2,1)} %param.25, bf16[2]{0:T(256)(128)(2,1)} %constant.11.clone), kind=kLoop, calls=%fused_computation.2 | loop fusion | flops 65536 | bytes 262148 | tf_op jit(solution)/shard_map/mul | solution.py:360
  5.8 0.8 copy.25
  6.6 1.6 %copy.35 = bf16[16,8,4,128]{3,1,2,0:T(8,128)(2,1)} copy(bf16[16,8,4,128]{3,2,1,0:T(4,128)(2,1)} %bitcast.14) | data formatting | bytes 262144
  8.2 0.6 concatenate.3.centre_ref
  8.8 1.6 %copy.26 = bf16[256,128]{0,1:T(8,128)(2,1)} copy(bf16[256,128]{1,0:T(8,128)(2,1)} %param.26) | data formatting | bytes 131072 | tf_op args[10]
  10.4 1.5 %copy.29 = bf16[96,128]{0,1:T(8,128)(2,1)} copy(bf16[96,128]{1,0:T(8,128)(2,1)} %param.30) | data formatting | bytes 49152 | tf_op args[14]
  11.8 1.3 %copy.30.pair_w_ref = f32[16,4]{1,0:T(8,128)} copy(bf16[16,4]{0,1:T(4,128)(2,1)} %param.22) | data formatting | bytes 384 | tf_op jit(solution)/shard_map/convert_element_type | solution.py:368
  13.2 1.2 %broadcast_in_dim.2.token_ref = s32[8,128]{1,0:T(8,128)} broadcast(s32[128]{0:T(128)} %param.18), dimensions={1} | broadcast | bytes 4608 | tf_op jit(solution)/shard_map/broadcast_in_dim | solution.py:367
  14.4 84.0 %diffusion_block.1 = (bf16[256,96]{1,0:T(8,128)(2,1)}, bf16[128,128]{1,0:T(8,128)(2,1)}) custom-call(bf16[256,128,128]{2,1,0:T(8,128)(2,1)} %pair_ref.1, bf16[144,128]{1,0:T(8,128)(2,1)} %concatenate.3.centre_ref, bf16[512,128]{1,0:T(8,128)(2,1)} %bitcast.15, bf16[128,256]{1,0:T(8,128)(2,1)} %bitcast.17, bf16[16,128]{1,0:T(8,128)(2,1)} %bitcast.19, ...), custom_call_target="tpu_custom_call" | custom-call | flops 7650410496 | bytes 10485760 | tf_op jit(solution)/shard_map/diffusion_block/pallas_call | solution.py:377
  98.4 1.6 %copy.31 = bf16[256,96]{0,1:T(8,128)(2,1)} copy(bf16[256,96]{1,0:T(8,128)(2,1)} %get-tuple-element.4) | data formatting | bytes 98304 | tf_op jit(solution)/shard_map/diffusion_block/pallas_call | solution.py:377
  99.9 1.4 %copy.37 = bf16[128,128]{1,0:T(8,128)(2,1)} copy(bf16[128,128]{1,0:T(8,128)(2,1)} %get-tuple-element.9) | data formatting | bytes 65536
  (1 shorter events, 0.0 us)

commit v3 on v2

--- a/solution.py
+++ b/solution.py
@@ -19,7 +19,7 @@
 RIM = (KW - QW) // 2
 LANES = 128
 ROWS_STEP = 16
-ROWS_CHAIN = 2
+ROWS_CHAIN = 4
 ATOM_STEP = 1
 TOKEN_STEP = 4
 MESH = pl.DeviceIdType.MESH
@@ -51,11 +51,11 @@
 
 def whole_kernel(
     peers, rows_n,
-    pair_ref, centre_ref, win_ref, wout_ref, bw_ref,
+    pair_ref, trans_in_ref, trans_out_ref, bw_ref,
     atoms_ref, atom_pair_ref, token_ref, single_ref, atom_w_ref, pair_w_ref, atom_wo_ref,
     agg_ref, token_w_ref, wo_ref, back_ref,
     single_out_ref, atoms_out_ref,
-    stage, send, bias_all, before, after, mid_all, token_all, hot, token_in, proj, kv_all,
+    centre_ref, win_ref, wout_ref, wo_t, back_t, stage, send, bias_all, before, after, mid_all, token_all, hot, token_in, proj, kv_all,
     part_send, part_all, pick_send, pick_all,
     halo_s, halo_r, tok_s, tok_r, mid_s, mid_r, kv_s, kv_r, bias_s, bias_r,
     part_s, part_r, pick_s, pick_r,
@@ -67,7 +67,7 @@
     width = pair_ref.shape[1]
     atom_count = atoms_ref.shape[0]
     query_rows = single_ref.shape[0]
-    own_cols = back_ref.shape[1]
+    own_cols = back_ref.shape[0]
 
     def other(k):
         return lax.rem(col + k, peers)
@@ -131,6 +131,26 @@
         def _():
             pl.semaphore_signal(barrier, inc=1, device_id=down, device_id_type=MESH)
 
+        spots = [lax.broadcasted_iota(jnp.int32, (CZ + 16, CZ), d) for d in (0, 1)]
+        mean_part = jnp.where(spots[0] < CZ, -1.0 / CZ, 1.0 / CZ)
+        centre_ref[...] = (jnp.where(spots[0] == spots[1], 1.0, 0.0) + mean_part).astype(
+            jnp.bfloat16
+        )
+        half = trans_in_ref.shape[2]
+        for m, scale in ((0, 0.5), (1, 1.0)):
+            block = trans_in_ref[:, m, :].astype(jnp.float32) * scale
+            win_ref[m * half : (m + 1) * half, :] = block.T.astype(jnp.bfloat16)
+        wout_ref[...] = trans_out_ref[...].astype(jnp.float32).T.astype(jnp.bfloat16)
+        back_t[...] = back_ref[...].astype(jnp.float32).T.astype(jnp.bfloat16)
+        wide = jnp.concatenate(
+            [
+                wo_ref[...].astype(jnp.float32),
+                jnp.zeros((LANES - own_cols, wo_ref.shape[1]), jnp.float32),
+            ]
+        )
+        wo_t[...] = wide.T.astype(jnp.bfloat16)
+        proj[...] = jnp.zeros_like(proj)
+
         extra = wraps_up.astype(jnp.int32) + wraps_down.astype(jnp.int32)
         pl.semaphore_wait(barrier, peers + rows_n - 2 + extra)
 
@@ -170,10 +190,13 @@
         extended = jnp.concatenate(
             [before[...].astype(jnp.float32), own, after[...].astype(jnp.float32)]
         )
-        projected = dot(layer_norm(extended).astype(jnp.bfloat16), atom_w_ref[...])
-        projected = projected.astype(jnp.bfloat16)
-        query = projected[RIM : RIM + atom_count, :CA]
-        gate = projected[RIM : RIM + atom_count, 3 * CA :].astype(jnp.float32)
+        normed = layer_norm(extended).astype(jnp.bfloat16)
+        query, key, value, gate = [
+            dot(normed, atom_w_ref[:, m, :]).astype(jnp.bfloat16) for m in range(4)
+        ]
+        query = query[RIM : RIM + atom_count]
+        gate = gate[RIM : RIM + atom_count].astype(jnp.float32)
+        factors = pair_w_ref[...].astype(jnp.float32)
         lane = lax.broadcasted_iota(jnp.int32, (QW, CA), 1)
         heads = [
             jnp.logical_and(lane >= h * ATOM_HEAD, lane < (h + 1) * ATOM_HEAD)
@@ -195,16 +218,16 @@
             ]
             bias = []
             for h in range(ATOM_HEADS):
-                total = planes[0] * pair_w_ref[0, h]
+                total = planes[0] * factors[h : h + 1, 0:1]
                 for c in range(1, len(planes)):
-                    total = total + planes[c] * pair_w_ref[c, h]
+                    total = total + planes[c] * factors[h : h + 1, c : c + 1]
                 bias.append(total)
-            scores = dot_rows(stacked, projected[low : low + KW, CA : 2 * CA])
+            scores = dot_rows(stacked, key[low : low + KW])
             scores = scores / math.sqrt(ATOM_HEAD) + jnp.concatenate(bias)
             place = spot + (start + low)
             inside = jnp.logical_and(place >= 0, place < all_atoms)
             weights = softmax_rows(jnp.where(inside, scores, masked_score))
-            mixed = dot(weights, projected[low : low + KW, 2 * CA : 3 * CA])
+            mixed = dot(weights, value[low : low + KW])
             picked = jnp.where(heads[0], mixed[:QW], 0.0)
             for h in range(1, ATOM_HEADS):
                 picked = picked + jnp.where(heads[h], mixed[h * QW : (h + 1) * QW], 0.0)
@@ -222,7 +245,7 @@
         slots = lax.broadcasted_iota(jnp.int32, (query_rows, LANES), 0) + row * query_rows
         counts = jnp.zeros((query_rows, LANES), jnp.float32)
         for c in range(peers):
-            match = (slots == token_all[c][0:1, :]).astype(jnp.float32)
+            match = (slots == token_all[c]).astype(jnp.float32)
             counts = counts + match
             hot[:, c * LANES : (c + 1) * LANES] = match.astype(jnp.bfloat16)
         count = jnp.sum(counts, axis=1, keepdims=True)
@@ -232,7 +255,9 @@
         held = (single_ref[...].astype(jnp.float32) + sums / count).astype(jnp.bfloat16)
         token_in[...] = held
         normed = layer_norm(held.astype(jnp.float32)).astype(jnp.bfloat16)
-        proj[...] = dot(normed, token_w_ref[...]).astype(jnp.bfloat16)
+        for m in range(4):
+            block = dot_rows(normed, token_w_ref[m]).astype(jnp.bfloat16)
+            proj[:, m * LANES : m * LANES + own_cols] = block
         kv_all[row] = proj[:, LANES : 3 * LANES]
         for k in range(1, rows_n):
             to_row(k, kv_all.at[row], kv_all.at[row]).start()
@@ -308,7 +333,7 @@
             attended = attended + jnp.where(mask, dot(weights, values), 0.0)
         gate = proj[:, 3 * LANES :].astype(jnp.float32)
         gated = (jax.nn.sigmoid(gate) * attended).astype(jnp.bfloat16)
-        part = dot_rows(wo_ref[...], gated).astype(jnp.bfloat16)
+        part = dot_rows(wo_t[...], gated).astype(jnp.bfloat16)
         part_send[...] = part.reshape(peers, own_cols, query_rows)
         for k in range(1, peers):
             to_col(k, part_send.at[other(k)], part_all.at[col], part_s, part_r).start()
@@ -324,15 +349,13 @@
             update = update + part_all[c].astype(jnp.float32)
         fresh = total + update
         single_t = fresh.astype(jnp.bfloat16)
-        back = dot(back_ref[...], single_t).astype(jnp.bfloat16)
+        back = dot(back_t[...], single_t).astype(jnp.bfloat16)
         picks = dot(back, hot[...]).astype(jnp.bfloat16)
         for c in range(peers):
             pick_send[c] = picks[:, c * LANES : (c + 1) * LANES]
         for k in range(1, peers):
             to_col(k, pick_send.at[other(k)], pick_all.at[col], pick_s, pick_r).start()
-        rest = LANES - own_cols
-        padded = jnp.concatenate([fresh, jnp.zeros((rest, query_rows), jnp.float32)])
-        single_out_ref[...] = padded.T[:, :own_cols].astype(jnp.bfloat16)
+        single_out_ref[...] = single_t
         pick_all[col] = pick_send[col]
         for k in range(1, peers):
             to_col(k, pick_send.at[other(k)], pick_all.at[source(k)], pick_s, pick_r).wait()
@@ -355,45 +378,41 @@
     width = single.shape[1]
     own_cols = token_wo.shape[0]
     bf16 = jnp.bfloat16
-    eye = jnp.eye(CZ, dtype=jnp.float32) - 1.0 / CZ
-    centre = jnp.concatenate([eye, jnp.full((16, CZ), 1.0 / CZ, jnp.float32)]).astype(bf16)
-    halved = trans_in * jnp.array([0.5, 1.0], bf16)[None, :, None]
-    win = halved.reshape(CZ, 2 * hidden).T
-    rest = LANES - own_cols
-    token_w_wide = jnp.pad(token_w, ((0, 0), (0, 0), (0, rest))).reshape(width, 4 * LANES)
-    wo_t = jnp.pad(token_wo, ((0, rest), (0, 0))).T
     operands = (
-        pair, centre, win, trans_out.T, bias_w.T,
-        atoms, atom_pair, jnp.broadcast_to(atom_token[None, :], (8, atom_count)), single,
-        atom_w.reshape(CA, 4 * CA), atom_pair_w.astype(jnp.float32), atom_wo, agg_w,
-        token_w_wide, wo_t, back_w.T,
+        pair, trans_in, trans_out, bias_w.T,
+        atoms, atom_pair, atom_token[None, :], single, atom_w, atom_pair_w.T, atom_wo, agg_w,
+        token_w.transpose(1, 2, 0), token_wo, back_w,
     )
     whole = lambda value: pl.BlockSpec(value.shape, lambda i, n=value.ndim: (0,) * n)
     in_specs = [pl.BlockSpec((ROWS_STEP, cols, CZ), lambda i: (i, 0, 0))]
     in_specs += [whole(value) for value in operands[1:]]
-    in_specs[10] = pl.BlockSpec(memory_space=pltpu.SMEM)
     dma = lambda n: pltpu.SemaphoreType.DMA((n,))
     p, r = peers - 1, rows_n - 1
-    return pl.pallas_call(
+    single_out, atoms_out = pl.pallas_call(
         functools.partial(whole_kernel, peers, rows_n),
         grid=(rows // ROWS_STEP,),
         out_shape=(
-            jax.ShapeDtypeStruct((rows, own_cols), bf16),
+            jax.ShapeDtypeStruct((own_cols, rows), bf16),
             jax.ShapeDtypeStruct((atom_count, CA), bf16),
         ),
         in_specs=in_specs,
         out_specs=(
-            pl.BlockSpec((rows, own_cols), lambda i: (0, 0)),
+            pl.BlockSpec((own_cols, rows), lambda i: (0, 0)),
             pl.BlockSpec((atom_count, CA), lambda i: (0, 0)),
         ),
         scratch_shapes=[
+            pltpu.VMEM((CZ + 16, CZ), bf16),
+            pltpu.VMEM((2 * hidden, CZ), bf16),
+            pltpu.VMEM((CZ, hidden), bf16),
+            pltpu.VMEM((width, LANES), bf16),
+            pltpu.VMEM((CA, own_cols), bf16),
             pltpu.VMEM((heads, ROWS_STEP, cols), jnp.float32),
             pltpu.VMEM((heads, rows, cols), bf16),
             pltpu.VMEM((peers, heads // peers, rows, cols), bf16),
             pltpu.VMEM((RIM, CA), bf16),
             pltpu.VMEM((RIM, CA), bf16),
             pltpu.VMEM((peers, atom_count, CA), bf16),
-            pltpu.VMEM((peers, 8, atom_count), jnp.int32),
+            pltpu.VMEM((peers, 1, atom_count), jnp.int32),
             pltpu.VMEM((rows, peers * atom_count), bf16),
             pltpu.VMEM((rows, width), bf16),
             pltpu.VMEM((rows, 4 * LANES), bf16),
@@ -416,6 +435,7 @@
         ),
         name="diffusion_block",
     )(*operands)
+    return single_out.T, atoms_out
 
 
 def solution(mesh):

time: 102 us -> 76.1 us (0.75)
  local copies, waits for them, and re-layouts: 15.6 us -> 2.8 us
  Pallas kernels: 84 us -> 72.4 us
  other arithmetic: 1.1 us -> 0 us
    pallas_call x1, Pallas kernels: 84 us -> 72.4 us  [body(): pl.pallas_call(functools.partial(whole_kernel, peers, rows_n), grid=(rows...]
    unnamed x5 -> x2, local copies, waits for them, and re-layouts: 7.04 us -> 2.8 us
    pallas_call x1 -> x0, local copies, waits for them, and re-layouts: 1.56 us -> none  [body(): pl.pallas_call(functools.partial(whole_kernel, peers, rows_n), grid=(rows...]
    convert_element_type x1 -> x0, local copies, waits for them, and re-layouts: 1.35 us -> none  [body(): atom_pair_w.astype(jnp.float32)]
    broadcast_in_dim x1 -> x0, local copies, waits for them, and re-layouts: 1.25 us -> none  [body(): jnp.broadcast_to(atom_token[None, :], (8, atom_count))]
    reshape x1 -> x0, local copies, waits for them, and re-layouts: 1.16 us -> none  [body(): jnp.pad(token_w, ((0, 0), (0, 0), (0, rest))).reshape(width, 4 * LANES)]
    pad x1 -> x0, local copies, waits for them, and re-layouts: 1.12 us -> none  [body(): jnp.pad(token_w, ((0, 0), (0, 0), (0, rest))).reshape(width, 4 * LANES)]
    mul x1 -> x0, other arithmetic: 1.08 us -> none  [body(): halved = trans_in * jnp.array([0.5, 1.0], bf16)[None, :, None]]
where the time goes in v3:
time: 76.1 us; the launch traced here: 75.8 us
  Pallas kernels  72.4 us (95%)
  local copies, waits for them, and re-layouts  2.8 us (4%)
    pallas_call x1, Pallas kernels, body(): pl.pallas_call(functools.partial(whole_kernel, peers, rows_n), grid=(rows...  72.4 us
    unnamed x2, local copies, waits for them, and re-layouts  2.8 us

profile of v3, /device:TPU:0, one launch (start us, length us, event | category | flops | bytes accessed | tf_op | source)
XLA Modules:
  0.0 75.8 jit_solution(83274079682990210)
XLA Ops:
  0.6 72.4 %diffusion_block.1 = (bf16[96,256]{1,0:T(8,128)(2,1)}, bf16[128,128]{1,0:T(8,128)(2,1)}) custom-call(bf16[256,128,128]{2,1,0:T(8,128)(2,1)} %pair_ref.1, bf16[128,2,256]{2,1,0:T(2,128)(2,1)} %trans_in_ref.1, bf16[256,128]{1,0:T(8,128)(2,1)} %trans_out_ref.1, bf16[16,128]{1,0:T(8,128)(2,1)} %bitcast.7, bf16[128,128]{1,0:T(8,128)(2,1)} %atoms_ref.1, ...), custom_call_target="tpu_custom_call" | custom-call | flops 7650410496 | bytes 10485760 | tf_op jit(solution)/shard_map/diffusion_block/pallas_call | solution.py:391
  73.0 1.4 %copy.19 = bf16[256,96]{0,1:T(8,128)(2,1)} copy(bf16[256,96]{0,1:T(8,128)(2,1)} %bitcast.5) | data formatting | bytes 98304
  74.5 1.4 %copy.20 = bf16[128,128]{1,0:T(8,128)(2,1)} copy(bf16[128,128]{1,0:T(8,128)(2,1)} %get-tuple-element.9) | data formatting | bytes 65536

commit v4 on v3

--- a/solution.py
+++ b/solution.py
@@ -18,10 +18,10 @@
 KW = 128
 RIM = (KW - QW) // 2
 LANES = 128
-ROWS_STEP = 16
+ROWS_STEP = 32
 ROWS_CHAIN = 4
 ATOM_STEP = 1
-TOKEN_STEP = 4
+TOKEN_STEP = 3
 MESH = pl.DeviceIdType.MESH
 
 
@@ -38,7 +38,7 @@
 def softmax_rows(scores):
     highest = jnp.max(scores, axis=-1, keepdims=True)
     raised = jnp.exp(scores - highest)
-    return (raised / jnp.sum(raised, axis=-1, keepdims=True)).astype(jnp.bfloat16)
+    return (raised * (1.0 / jnp.sum(raised, axis=-1, keepdims=True))).astype(jnp.bfloat16)
 
 
 def dot(a, b):
@@ -223,7 +223,7 @@
                     total = total + planes[c] * factors[h : h + 1, c : c + 1]
                 bias.append(total)
             scores = dot_rows(stacked, key[low : low + KW])
-            scores = scores / math.sqrt(ATOM_HEAD) + jnp.concatenate(bias)
+            scores = scores * (1.0 / math.sqrt(ATOM_HEAD)) + jnp.concatenate(bias)
             place = spot + (start + low)
             inside = jnp.logical_and(place >= 0, place < all_atoms)
             weights = softmax_rows(jnp.where(inside, scores, masked_score))
@@ -252,7 +252,7 @@
         mids = mid_all[...].reshape(peers * atom_count, CA)
         features = jnp.maximum(dot(mids, agg_ref[...]), 0.0).astype(jnp.bfloat16)
         sums = dot(hot[...], features)
-        held = (single_ref[...].astype(jnp.float32) + sums / count).astype(jnp.bfloat16)
+        held = (single_ref[...].astype(jnp.float32) + sums * (1.0 / count)).astype(jnp.bfloat16)
         token_in[...] = held
         normed = layer_norm(held.astype(jnp.float32)).astype(jnp.bfloat16)
         for m in range(4):
@@ -329,7 +329,7 @@
             mask = jnp.logical_and(lane >= h * HEAD, lane < (h + 1) * HEAD)
             scores = dot_rows(jnp.where(mask, query, 0.0).astype(jnp.bfloat16), keys)
             bias = jnp.concatenate([bias_all[c, h] for c in range(peers)], axis=1)
-            weights = softmax_rows(scores / math.sqrt(HEAD) + bias.astype(jnp.float32))
+            weights = softmax_rows(scores * (1.0 / math.sqrt(HEAD)) + bias.astype(jnp.float32))
             attended = attended + jnp.where(mask, dot(weights, values), 0.0)
         gate = proj[:, 3 * LANES :].astype(jnp.float32)
         gated = (jax.nn.sigmoid(gate) * attended).astype(jnp.bfloat16)

time: 76.1 us -> 69.9 us (0.919)
  Pallas kernels: 72.4 us -> 66.2 us
    pallas_call x1, Pallas kernels: 72.4 us -> 66.2 us  [body(): pl.pallas_call(functools.partial(whole_kernel, peers, rows_n), grid=(rows...]
where the time goes in v4:
time: 69.9 us; the launch traced here: 69.6 us
  Pallas kernels  66.2 us (95%)
  local copies, waits for them, and re-layouts  2.8 us (4%)
    pallas_call x1, Pallas kernels, body(): pl.pallas_call(functools.partial(whole_kernel, peers, rows_n), grid=(rows...  66.2 us
    unnamed x2, local copies, waits for them, and re-layouts  2.8 us

profile of v4, /device:TPU:0, one launch (start us, length us, event | category | flops | bytes accessed | tf_op | source)
XLA Modules:
  0.0 69.6 jit_solution(1241247463870119974)
XLA Ops:
  0.6 66.2 %diffusion_block.1 = (bf16[96,256]{1,0:T(8,128)(2,1)}, bf16[128,128]{1,0:T(8,128)(2,1)}) custom-call(bf16[256,128,128]{2,1,0:T(8,128)(2,1)} %pair_ref.1, bf16[128,2,256]{2,1,0:T(2,128)(2,1)} %trans_in_ref.1, bf16[256,128]{1,0:T(8,128)(2,1)} %trans_out_ref.1, bf16[16,128]{1,0:T(8,128)(2,1)} %bitcast.7, bf16[128,128]{1,0:T(8,128)(2,1)} %atoms_ref.1, ...), custom_call_target="tpu_custom_call" | custom-call | flops 7650410496 | bytes 10485760 | tf_op jit(solution)/shard_map/diffusion_block/pallas_call | solution.py:391
  66.8 1.4 %copy.19 = bf16[256,96]{0,1:T(8,128)(2,1)} copy(bf16[256,96]{0,1:T(8,128)(2,1)} %bitcast.5) | data formatting | bytes 98304
  68.2 1.4 %copy.20 = bf16[128,128]{1,0:T(8,128)(2,1)} copy(bf16[128,128]{1,0:T(8,128)(2,1)} %get-tuple-element.9) | data formatting | bytes 65536

commit v5 on v4

--- a/solution.py
+++ b/solution.py
@@ -22,6 +22,9 @@
 ROWS_CHAIN = 4
 ATOM_STEP = 1
 TOKEN_STEP = 3
+BLOCK_ROWS = 64
+ATTEND_STEPS = (4, 5, 7)
+FINISH_STEPS = (6, 7)
 MESH = pl.DeviceIdType.MESH
 
 
@@ -55,7 +58,7 @@
     atoms_ref, atom_pair_ref, token_ref, single_ref, atom_w_ref, pair_w_ref, atom_wo_ref,
     agg_ref, token_w_ref, wo_ref, back_ref,
     single_out_ref, atoms_out_ref,
-    centre_ref, win_ref, wout_ref, wo_t, back_t, stage, send, bias_all, before, after, mid_all, token_all, hot, token_in, proj, kv_all,
+    centre_ref, win_ref, wout_ref, wo_wide, back_t, own_in, single_rows, stage, send, bias_all, before, after, mid_all, token_all, hot, proj, kv_all,
     part_send, part_all, pick_send, pick_all,
     halo_s, halo_r, tok_s, tok_r, mid_s, mid_r, kv_s, kv_r, bias_s, bias_r,
     part_s, part_r, pick_s, pick_r,
@@ -81,10 +84,10 @@
     def source_row(k):
         return lax.rem(row + rows_n - k, rows_n)
 
-    def to_col(k, src, dst, s, r):
+    def to_col(k, src, dst, s, r, base=0):
         return pltpu.make_async_remote_copy(
-            src_ref=src, dst_ref=dst, send_sem=s.at[k - 1], recv_sem=r.at[k - 1],
-            device_id=(row, other(k)), device_id_type=MESH,
+            src_ref=src, dst_ref=dst, send_sem=s.at[base + k - 1],
+            recv_sem=r.at[base + k - 1], device_id=(row, other(k)), device_id_type=MESH,
         )
 
     def to_row(k, src, dst):
@@ -141,14 +144,13 @@
             block = trans_in_ref[:, m, :].astype(jnp.float32) * scale
             win_ref[m * half : (m + 1) * half, :] = block.T.astype(jnp.bfloat16)
         wout_ref[...] = trans_out_ref[...].astype(jnp.float32).T.astype(jnp.bfloat16)
-        back_t[...] = back_ref[...].astype(jnp.float32).T.astype(jnp.bfloat16)
-        wide = jnp.concatenate(
-            [
-                wo_ref[...].astype(jnp.float32),
-                jnp.zeros((LANES - own_cols, wo_ref.shape[1]), jnp.float32),
-            ]
-        )
-        wo_t[...] = wide.T.astype(jnp.bfloat16)
+        back_t[...] = jnp.zeros_like(back_t)
+        back_t[:, :own_cols] = back_ref[...].astype(jnp.float32).T.astype(jnp.bfloat16)
+        wo_wide[...] = jnp.zeros_like(wo_wide)
+        plain = wo_ref[...].astype(jnp.float32)
+        for c in range(peers):
+            block = plain[:, c * own_cols : (c + 1) * own_cols]
+            wo_wide[:own_cols, c * LANES : c * LANES + own_cols] = block.astype(jnp.bfloat16)
         proj[...] = jnp.zeros_like(proj)
 
         extra = wraps_up.astype(jnp.int32) + wraps_down.astype(jnp.int32)
@@ -253,7 +255,12 @@
         features = jnp.maximum(dot(mids, agg_ref[...]), 0.0).astype(jnp.bfloat16)
         sums = dot(hot[...], features)
         held = (single_ref[...].astype(jnp.float32) + sums * (1.0 / count)).astype(jnp.bfloat16)
-        token_in[...] = held
+        spot = lax.broadcasted_iota(jnp.int32, (held.shape[1], LANES), 0) - col * own_cols
+        column = lax.broadcasted_iota(jnp.int32, (held.shape[1], LANES), 1)
+        chosen = jnp.logical_and(spot == column, column < own_cols)
+        own_in[...] = dot(held, chosen.astype(jnp.float32).astype(jnp.bfloat16)).astype(
+            jnp.bfloat16
+        )
         normed = layer_norm(held.astype(jnp.float32)).astype(jnp.bfloat16)
         for m in range(4):
             block = dot_rows(normed, token_w_ref[m]).astype(jnp.bfloat16)
@@ -261,6 +268,70 @@
         kv_all[row] = proj[:, LANES : 3 * LANES]
         for k in range(1, rows_n):
             to_row(k, kv_all.at[row], kv_all.at[row]).start()
+
+    block_steps = BLOCK_ROWS // ROWS_STEP
+    blocks = query_rows // BLOCK_ROWS
+    near = peers - 1
+
+    def attend(b):
+        part_rows = pl.ds(b * BLOCK_ROWS, BLOCK_ROWS)
+        if b == 0:
+            for k in range(1, rows_n):
+                to_row(k, kv_all.at[row], kv_all.at[source_row(k)]).wait()
+        for k in range(1, peers):
+            to_col(
+                k, send.at[pl.ds(other(k) * group, group), part_rows, :],
+                bias_all.at[source(k), :, part_rows, :], bias_s, bias_r, b * near,
+            ).wait()
+        query = proj[part_rows, :LANES].astype(jnp.float32)
+        keys = kv_all[:, :, :LANES].reshape(rows_n * query_rows, LANES)
+        values = kv_all[:, :, LANES:].reshape(rows_n * query_rows, LANES)
+        lane = lax.broadcasted_iota(jnp.int32, (BLOCK_ROWS, LANES), 1)
+        masks = [
+            jnp.logical_and(lane >= h * HEAD, lane < (h + 1) * HEAD) for h in range(group)
+        ]
+        stacked = jnp.concatenate([jnp.where(mask, query, 0.0) for mask in masks])
+        scores = dot_rows(stacked.astype(jnp.bfloat16), keys) * (1.0 / math.sqrt(HEAD))
+        bias = jnp.concatenate(
+            [
+                jnp.concatenate([bias_all[c, h, part_rows, :] for c in range(peers)], axis=1)
+                for h in range(group)
+            ]
+        )
+        mixed = dot(softmax_rows(scores + bias.astype(jnp.float32)), values)
+        attended = jnp.where(masks[0], mixed[:BLOCK_ROWS], 0.0)
+        for h in range(1, group):
+            attended = attended + jnp.where(
+                masks[h], mixed[h * BLOCK_ROWS : (h + 1) * BLOCK_ROWS], 0.0
+            )
+        gate = proj[part_rows, 3 * LANES :].astype(jnp.float32)
+        gated = (jax.nn.sigmoid(gate) * attended).astype(jnp.bfloat16)
+        part = dot(gated, wo_wide[...]).astype(jnp.bfloat16)
+        for c in range(peers):
+            part_send[b, c] = part[:, c * LANES : (c + 1) * LANES]
+        for k in range(1, peers):
+            to_col(
+                k, part_send.at[b, other(k)], part_all.at[b, col], part_s, part_r, b * near
+            ).start()
+        part_all[b, col] = part_send[b, col]
+
+    def finish(b):
+        for k in range(1, peers):
+            to_col(
+                k, part_send.at[b, other(k)], part_all.at[b, source(k)], part_s, part_r, b * near
+            ).wait()
+        update = part_all[b, 0].astype(jnp.float32)
+        for c in range(1, peers):
+            update = update + part_all[b, c].astype(jnp.float32)
+        part_rows = pl.ds(b * BLOCK_ROWS, BLOCK_ROWS)
+        total = own_in[part_rows, :].astype(jnp.float32) + update
+        single_rows[part_rows, :] = total.astype(jnp.bfloat16)
+
+    for b, at in enumerate(ATTEND_STEPS):
+        pl.when(step == at)(functools.partial(attend, b))
+
+    for b, at in enumerate(FINISH_STEPS):
+        pl.when(step == at)(functools.partial(finish, b))
 
     def first(k):
         x = pair_ref[k * ROWS_CHAIN : (k + 1) * ROWS_CHAIN].reshape(ROWS_CHAIN * width, CZ)
@@ -309,53 +380,24 @@
     for k in range(1, peers):
         to_col(
             k, send.at[pl.ds(other(k) * group, group), rows, :], bias_all.at[col, :, rows, :],
-            bias_s, bias_r,
+            bias_s, bias_r, (step // block_steps) * near,
         ).start()
 
     @pl.when(step == steps - 1)
     def _():
-        for k in range(1, rows_n):
-            to_row(k, kv_all.at[row], kv_all.at[source_row(k)]).wait()
-        for k in range(1, peers):
-            to_col(
-                k, send.at[pl.ds(other(k) * group, group)], bias_all.at[source(k)], bias_s, bias_r
-            ).wait()
-        query = proj[:, :LANES].astype(jnp.float32)
-        keys = kv_all[:, :, :LANES].reshape(rows_n * query_rows, LANES)
-        values = kv_all[:, :, LANES:].reshape(rows_n * query_rows, LANES)
-        lane = lax.broadcasted_iota(jnp.int32, (query_rows, LANES), 1)
-        attended = jnp.zeros((query_rows, LANES), jnp.float32)
-        for h in range(group):
-            mask = jnp.logical_and(lane >= h * HEAD, lane < (h + 1) * HEAD)
-            scores = dot_rows(jnp.where(mask, query, 0.0).astype(jnp.bfloat16), keys)
-            bias = jnp.concatenate([bias_all[c, h] for c in range(peers)], axis=1)
-            weights = softmax_rows(scores * (1.0 / math.sqrt(HEAD)) + bias.astype(jnp.float32))
-            attended = attended + jnp.where(mask, dot(weights, values), 0.0)
-        gate = proj[:, 3 * LANES :].astype(jnp.float32)
-        gated = (jax.nn.sigmoid(gate) * attended).astype(jnp.bfloat16)
-        part = dot_rows(wo_t[...], gated).astype(jnp.bfloat16)
-        part_send[...] = part.reshape(peers, own_cols, query_rows)
-        for k in range(1, peers):
-            to_col(k, part_send.at[other(k)], part_all.at[col], part_s, part_r).start()
-        spot = lax.broadcasted_iota(jnp.int32, (own_cols, token_in.shape[1]), 0) + col * own_cols
-        column = lax.broadcasted_iota(jnp.int32, (own_cols, token_in.shape[1]), 1)
-        chosen = (spot == column).astype(jnp.float32).astype(jnp.bfloat16)
-        total = dot_rows(chosen, token_in[...])
-        part_all[col] = part_send[col]
-        for k in range(1, peers):
-            to_col(k, part_send.at[other(k)], part_all.at[source(k)], part_s, part_r).wait()
-        update = part_all[0].astype(jnp.float32)
-        for c in range(1, peers):
-            update = update + part_all[c].astype(jnp.float32)
-        fresh = total + update
-        single_t = fresh.astype(jnp.bfloat16)
-        back = dot(back_t[...], single_t).astype(jnp.bfloat16)
+        for b in range(len(FINISH_STEPS), len(ATTEND_STEPS)):
+            finish(b)
+        for b in range(len(ATTEND_STEPS), blocks):
+            attend(b)
+        for b in range(len(ATTEND_STEPS), blocks):
+            finish(b)
+        back = dot_rows(back_t[...], single_rows[...]).astype(jnp.bfloat16)
         picks = dot(back, hot[...]).astype(jnp.bfloat16)
         for c in range(peers):
             pick_send[c] = picks[:, c * LANES : (c + 1) * LANES]
         for k in range(1, peers):
             to_col(k, pick_send.at[other(k)], pick_all.at[col], pick_s, pick_r).start()
-        single_out_ref[...] = single_t
+        single_out_ref[...] = single_rows[:, :own_cols]
         pick_all[col] = pick_send[col]
         for k in range(1, peers):
             to_col(k, pick_send.at[other(k)], pick_all.at[source(k)], pick_s, pick_r).wait()
@@ -388,24 +430,27 @@
     in_specs += [whole(value) for value in operands[1:]]
     dma = lambda n: pltpu.SemaphoreType.DMA((n,))
     p, r = peers - 1, rows_n - 1
+    blocks = rows // BLOCK_ROWS
     single_out, atoms_out = pl.pallas_call(
         functools.partial(whole_kernel, peers, rows_n),
         grid=(rows // ROWS_STEP,),
         out_shape=(
-            jax.ShapeDtypeStruct((own_cols, rows), bf16),
+            jax.ShapeDtypeStruct((rows, own_cols), bf16),
             jax.ShapeDtypeStruct((atom_count, CA), bf16),
         ),
         in_specs=in_specs,
         out_specs=(
-            pl.BlockSpec((own_cols, rows), lambda i: (0, 0)),
+            pl.BlockSpec((rows, own_cols), lambda i: (0, 0)),
             pl.BlockSpec((atom_count, CA), lambda i: (0, 0)),
         ),
         scratch_shapes=[
             pltpu.VMEM((CZ + 16, CZ), bf16),
             pltpu.VMEM((2 * hidden, CZ), bf16),
             pltpu.VMEM((CZ, hidden), bf16),
-            pltpu.VMEM((width, LANES), bf16),
-            pltpu.VMEM((CA, own_cols), bf16),
+            pltpu.VMEM((LANES, peers * LANES), bf16),
+            pltpu.VMEM((CA, LANES), bf16),
+            pltpu.VMEM((rows, LANES), bf16),
+            pltpu.VMEM((rows, LANES), bf16),
             pltpu.VMEM((heads, ROWS_STEP, cols), jnp.float32),
             pltpu.VMEM((heads, rows, cols), bf16),
             pltpu.VMEM((peers, heads // peers, rows, cols), bf16),
@@ -414,15 +459,14 @@
             pltpu.VMEM((peers, atom_count, CA), bf16),
             pltpu.VMEM((peers, 1, atom_count), jnp.int32),
             pltpu.VMEM((rows, peers * atom_count), bf16),
-            pltpu.VMEM((rows, width), bf16),
             pltpu.VMEM((rows, 4 * LANES), bf16),
             pltpu.VMEM((rows_n, rows, 2 * LANES), bf16),
-            pltpu.VMEM((peers, own_cols, rows), bf16),
-            pltpu.VMEM((peers, own_cols, rows), bf16),
+            pltpu.VMEM((blocks, peers, BLOCK_ROWS, LANES), bf16),
+            pltpu.VMEM((blocks, peers, BLOCK_ROWS, LANES), bf16),
             pltpu.VMEM((peers, CA, atom_count), bf16),
             pltpu.VMEM((peers, CA, atom_count), bf16),
-            dma(2), dma(2), dma(p), dma(p), dma(p), dma(p), dma(r), dma(r), dma(p), dma(p),
-            dma(p), dma(p), dma(p), dma(p),
+            dma(2), dma(2), dma(p), dma(p), dma(p), dma(p), dma(r), dma(r),
+            dma(blocks * p), dma(blocks * p), dma(blocks * p), dma(blocks * p), dma(p), dma(p),
         ],
         compiler_params=pltpu.CompilerParams(
             collective_id=0, has_side_effects=True, vmem_limit_bytes=56 * 2**20,
@@ -435,7 +479,7 @@
         ),
         name="diffusion_block",
     )(*operands)
-    return single_out.T, atoms_out
+    return single_out, atoms_out
 
 
 def solution(mesh):

time: 69.9 us -> 72.9 us (1.043)
  Pallas kernels: 66.2 us -> 69.1 us
    pallas_call x1, Pallas kernels: 66.2 us -> 69.1 us  [body(): pl.pallas_call(functools.partial(whole_kernel, peers, rows_n), grid=(rows...]
    pallas_call x0 -> x1, local copies, waits for them, and re-layouts: none -> 1.56 us  [body(): pl.pallas_call(functools.partial(whole_kernel, peers, rows_n), grid=(rows...]
    unnamed x2 -> x1, local copies, waits for them, and re-layouts: 2.8 us -> 1.37 us
where the time goes in v5:
time: 72.9 us; the launch traced here: 72.7 us
  Pallas kernels  69.1 us (95%)
  local copies, waits for them, and re-layouts  2.93 us (4%)
    pallas_call x1, Pallas kernels, body(): pl.pallas_call(functools.partial(whole_kernel, peers, rows_n), grid=(rows...  69.1 us
    pallas_call x1, local copies, waits for them, and re-layouts, body(): pl.pallas_call(functools.partial(whole_kernel, peers, rows_n), grid=(rows...  1.56 us

profile of v5, /device:TPU:0, one launch (start us, length us, event | category | flops | bytes accessed | tf_op | source)
XLA Modules:
  0.0 72.7 jit_solution(10821801913608768554)
XLA Ops:
  0.6 69.1 %diffusion_block.1 = (bf16[256,96]{1,0:T(8,128)(2,1)}, bf16[128,128]{1,0:T(8,128)(2,1)}) custom-call(bf16[256,128,128]{2,1,0:T(8,128)(2,1)} %pair_ref.1, bf16[128,2,256]{2,1,0:T(2,128)(2,1)} %trans_in_ref.1, bf16[256,128]{1,0:T(8,128)(2,1)} %trans_out_ref.1, bf16[16,128]{1,0:T(8,128)(2,1)} %bitcast.5, bf16[128,128]{1,0:T(8,128)(2,1)} %atoms_ref.1, ...), custom_call_target="tpu_custom_call" | custom-call | flops 7650410496 | bytes 10485760 | tf_op jit(solution)/shard_map/diffusion_block/pallas_call | solution.py:434
  69.7 1.6 %copy.17 = bf16[256,96]{0,1:T(8,128)(2,1)} copy(bf16[256,96]{1,0:T(8,128)(2,1)} %get-tuple-element.2) | data formatting | bytes 98304 | tf_op jit(solution)/shard_map/diffusion_block/pallas_call | solution.py:434
  71.3 1.4 %copy.19 = bf16[128,128]{1,0:T(8,128)(2,1)} copy(bf16[128,128]{1,0:T(8,128)(2,1)} %get-tuple-element.7) | data formatting | bytes 65536

commit v6 on v4

--- a/solution.py
+++ b/solution.py
@@ -19,9 +19,9 @@
 RIM = (KW - QW) // 2
 LANES = 128
 ROWS_STEP = 32
-ROWS_CHAIN = 4
-ATOM_STEP = 1
-TOKEN_STEP = 3
+ROWS_CHAIN = 8
+ATOM_STEP = 2
+TOKEN_STEP = 5
 MESH = pl.DeviceIdType.MESH
 
 

time: 69.9 us -> 65.4 us (0.936)
  Pallas kernels: 66.2 us -> 61.7 us
    pallas_call x1, Pallas kernels: 66.2 us -> 61.7 us  [body(): pl.pallas_call(functools.partial(whole_kernel, peers, rows_n), grid=(rows...]
where the time goes in v6:
time: 65.4 us; the launch traced here: 65.1 us
  Pallas kernels  61.7 us (94%)
  local copies, waits for them, and re-layouts  2.8 us (4%)
    pallas_call x1, Pallas kernels, body(): pl.pallas_call(functools.partial(whole_kernel, peers, rows_n), grid=(rows...  61.7 us
    unnamed x2, local copies, waits for them, and re-layouts  2.8 us

profile of v6, /device:TPU:0, one launch (start us, length us, event | category | flops | bytes accessed | tf_op | source)
XLA Modules:
  0.0 65.1 jit_solution(9726187755599751734)
XLA Ops:
  0.6 61.7 %diffusion_block.1 = (bf16[96,256]{1,0:T(8,128)(2,1)}, bf16[128,128]{1,0:T(8,128)(2,1)}) custom-call(bf16[256,128,128]{2,1,0:T(8,128)(2,1)} %pair_ref.1, bf16[128,2,256]{2,1,0:T(2,128)(2,1)} %trans_in_ref.1, bf16[256,128]{1,0:T(8,128)(2,1)} %trans_out_ref.1, bf16[16,128]{1,0:T(8,128)(2,1)} %bitcast.7, bf16[128,128]{1,0:T(8,128)(2,1)} %atoms_ref.1, ...), custom_call_target="tpu_custom_call" | custom-call | flops 7650410496 | bytes 10485760 | tf_op jit(solution)/shard_map/diffusion_block/pallas_call | solution.py:391
  62.3 1.4 %copy.19 = bf16[256,96]{0,1:T(8,128)(2,1)} copy(bf16[256,96]{0,1:T(8,128)(2,1)} %bitcast.5) | data formatting | bytes 98304
  63.7 1.4 %copy.20 = bf16[128,128]{1,0:T(8,128)(2,1)} copy(bf16[128,128]{1,0:T(8,128)(2,1)} %get-tuple-element.9) | data formatting | bytes 65536

commit v7 on v5

--- a/solution.py
+++ b/solution.py
@@ -19,12 +19,10 @@
 RIM = (KW - QW) // 2
 LANES = 128
 ROWS_STEP = 32
-ROWS_CHAIN = 4
-ATOM_STEP = 1
-TOKEN_STEP = 3
-BLOCK_ROWS = 64
-ATTEND_STEPS = (4, 5, 7)
-FINISH_STEPS = (6, 7)
+ROWS_CHAIN = 8
+ATOM_STEP = 2
+TOKEN_STEP = 5
+BLOCK_ROWS = 128
 MESH = pl.DeviceIdType.MESH
 
 
@@ -58,7 +56,7 @@
     atoms_ref, atom_pair_ref, token_ref, single_ref, atom_w_ref, pair_w_ref, atom_wo_ref,
     agg_ref, token_w_ref, wo_ref, back_ref,
     single_out_ref, atoms_out_ref,
-    centre_ref, win_ref, wout_ref, wo_wide, back_t, own_in, single_rows, stage, send, bias_all, before, after, mid_all, token_all, hot, proj, kv_all,
+    centre_ref, win_ref, wout_ref, wo_t, back_t, stage, send, bias_all, before, after, mid_all, token_all, hot, token_in, proj, kv_all,
     part_send, part_all, pick_send, pick_all,
     halo_s, halo_r, tok_s, tok_r, mid_s, mid_r, kv_s, kv_r, bias_s, bias_r,
     part_s, part_r, pick_s, pick_r,
@@ -144,13 +142,14 @@
             block = trans_in_ref[:, m, :].astype(jnp.float32) * scale
             win_ref[m * half : (m + 1) * half, :] = block.T.astype(jnp.bfloat16)
         wout_ref[...] = trans_out_ref[...].astype(jnp.float32).T.astype(jnp.bfloat16)
-        back_t[...] = jnp.zeros_like(back_t)
-        back_t[:, :own_cols] = back_ref[...].astype(jnp.float32).T.astype(jnp.bfloat16)
-        wo_wide[...] = jnp.zeros_like(wo_wide)
-        plain = wo_ref[...].astype(jnp.float32)
-        for c in range(peers):
-            block = plain[:, c * own_cols : (c + 1) * own_cols]
-            wo_wide[:own_cols, c * LANES : c * LANES + own_cols] = block.astype(jnp.bfloat16)
+        back_t[...] = back_ref[...].astype(jnp.float32).T.astype(jnp.bfloat16)
+        wide = jnp.concatenate(
+            [
+                wo_ref[...].astype(jnp.float32),
+                jnp.zeros((LANES - own_cols, wo_ref.shape[1]), jnp.float32),
+            ]
+        )
+        wo_t[...] = wide.T.astype(jnp.bfloat16)
         proj[...] = jnp.zeros_like(proj)
 
         extra = wraps_up.astype(jnp.int32) + wraps_down.astype(jnp.int32)
@@ -255,12 +254,7 @@
         features = jnp.maximum(dot(mids, agg_ref[...]), 0.0).astype(jnp.bfloat16)
         sums = dot(hot[...], features)
         held = (single_ref[...].astype(jnp.float32) + sums * (1.0 / count)).astype(jnp.bfloat16)
-        spot = lax.broadcasted_iota(jnp.int32, (held.shape[1], LANES), 0) - col * own_cols
-        column = lax.broadcasted_iota(jnp.int32, (held.shape[1], LANES), 1)
-        chosen = jnp.logical_and(spot == column, column < own_cols)
-        own_in[...] = dot(held, chosen.astype(jnp.float32).astype(jnp.bfloat16)).astype(
-            jnp.bfloat16
-        )
+        token_in[...] = held
         normed = layer_norm(held.astype(jnp.float32)).astype(jnp.bfloat16)
         for m in range(4):
             block = dot_rows(normed, token_w_ref[m]).astype(jnp.bfloat16)
@@ -275,9 +269,6 @@
 
     def attend(b):
         part_rows = pl.ds(b * BLOCK_ROWS, BLOCK_ROWS)
-        if b == 0:
-            for k in range(1, rows_n):
-                to_row(k, kv_all.at[row], kv_all.at[source_row(k)]).wait()
         for k in range(1, peers):
             to_col(
                 k, send.at[pl.ds(other(k) * group, group), part_rows, :],
@@ -306,16 +297,15 @@
             )
         gate = proj[part_rows, 3 * LANES :].astype(jnp.float32)
         gated = (jax.nn.sigmoid(gate) * attended).astype(jnp.bfloat16)
-        part = dot(gated, wo_wide[...]).astype(jnp.bfloat16)
-        for c in range(peers):
-            part_send[b, c] = part[:, c * LANES : (c + 1) * LANES]
+        part = dot_rows(wo_t[...], gated).astype(jnp.bfloat16)
+        part_send[b] = part.reshape(peers, own_cols, BLOCK_ROWS)
         for k in range(1, peers):
             to_col(
                 k, part_send.at[b, other(k)], part_all.at[b, col], part_s, part_r, b * near
             ).start()
         part_all[b, col] = part_send[b, col]
 
-    def finish(b):
+    def summed(b):
         for k in range(1, peers):
             to_col(
                 k, part_send.at[b, other(k)], part_all.at[b, source(k)], part_s, part_r, b * near
@@ -323,15 +313,7 @@
         update = part_all[b, 0].astype(jnp.float32)
         for c in range(1, peers):
             update = update + part_all[b, c].astype(jnp.float32)
-        part_rows = pl.ds(b * BLOCK_ROWS, BLOCK_ROWS)
-        total = own_in[part_rows, :].astype(jnp.float32) + update
-        single_rows[part_rows, :] = total.astype(jnp.bfloat16)
-
-    for b, at in enumerate(ATTEND_STEPS):
-        pl.when(step == at)(functools.partial(attend, b))
-
-    for b, at in enumerate(FINISH_STEPS):
-        pl.when(step == at)(functools.partial(finish, b))
+        return update
 
     def first(k):
         x = pair_ref[k * ROWS_CHAIN : (k + 1) * ROWS_CHAIN].reshape(ROWS_CHAIN * width, CZ)
@@ -385,19 +367,24 @@
 
     @pl.when(step == steps - 1)
     def _():
-        for b in range(len(FINISH_STEPS), len(ATTEND_STEPS)):
-            finish(b)
-        for b in range(len(ATTEND_STEPS), blocks):
+        for k in range(1, rows_n):
+            to_row(k, kv_all.at[row], kv_all.at[source_row(k)]).wait()
+        for b in range(blocks):
             attend(b)
-        for b in range(len(ATTEND_STEPS), blocks):
-            finish(b)
-        back = dot_rows(back_t[...], single_rows[...]).astype(jnp.bfloat16)
+        spot = lax.broadcasted_iota(jnp.int32, (own_cols, token_in.shape[1]), 0) + col * own_cols
+        column = lax.broadcasted_iota(jnp.int32, (own_cols, token_in.shape[1]), 1)
+        chosen = (spot == column).astype(jnp.float32).astype(jnp.bfloat16)
+        total = dot_rows(chosen, token_in[...])
+        update = jnp.concatenate([summed(b) for b in range(blocks)], axis=1)
+        fresh = total + update
+        single_t = fresh.astype(jnp.bfloat16)
+        back = dot(back_t[...], single_t).astype(jnp.bfloat16)
         picks = dot(back, hot[...]).astype(jnp.bfloat16)
         for c in range(peers):
             pick_send[c] = picks[:, c * LANES : (c + 1) * LANES]
         for k in range(1, peers):
             to_col(k, pick_send.at[other(k)], pick_all.at[col], pick_s, pick_r).start()
-        single_out_ref[...] = single_rows[:, :own_cols]
+        single_out_ref[...] = single_t
         pick_all[col] = pick_send[col]
         for k in range(1, peers):
             to_col(k, pick_send.at[other(k)], pick_all.at[source(k)], pick_s, pick_r).wait()
@@ -435,22 +422,20 @@
         functools.partial(whole_kernel, peers, rows_n),
         grid=(rows // ROWS_STEP,),
         out_shape=(
-            jax.ShapeDtypeStruct((rows, own_cols), bf16),
+            jax.ShapeDtypeStruct((own_cols, rows), bf16),
             jax.ShapeDtypeStruct((atom_count, CA), bf16),
         ),
         in_specs=in_specs,
         out_specs=(
-            pl.BlockSpec((rows, own_cols), lambda i: (0, 0)),
+            pl.BlockSpec((own_cols, rows), lambda i: (0, 0)),
             pl.BlockSpec((atom_count, CA), lambda i: (0, 0)),
         ),
         scratch_shapes=[
             pltpu.VMEM((CZ + 16, CZ), bf16),
             pltpu.VMEM((2 * hidden, CZ), bf16),
             pltpu.VMEM((CZ, hidden), bf16),
-            pltpu.VMEM((LANES, peers * LANES), bf16),
-            pltpu.VMEM((CA, LANES), bf16),
-            pltpu.VMEM((rows, LANES), bf16),
-            pltpu.VMEM((rows, LANES), bf16),
+            pltpu.VMEM((width, LANES), bf16),
+            pltpu.VMEM((CA, own_cols), bf16),
             pltpu.VMEM((heads, ROWS_STEP, cols), jnp.float32),
             pltpu.VMEM((heads, rows, cols), bf16),
             pltpu.VMEM((peers, heads // peers, rows, cols), bf16),
@@ -459,10 +444,11 @@
             pltpu.VMEM((peers, atom_count, CA), bf16),
             pltpu.VMEM((peers, 1, atom_count), jnp.int32),
             pltpu.VMEM((rows, peers * atom_count), bf16),
+            pltpu.VMEM((rows, width), bf16),
             pltpu.VMEM((rows, 4 * LANES), bf16),
             pltpu.VMEM((rows_n, rows, 2 * LANES), bf16),
-            pltpu.VMEM((blocks, peers, BLOCK_ROWS, LANES), bf16),
-            pltpu.VMEM((blocks, peers, BLOCK_ROWS, LANES), bf16),
+            pltpu.VMEM((blocks, peers, own_cols, BLOCK_ROWS), bf16),
+            pltpu.VMEM((blocks, peers, own_cols, BLOCK_ROWS), bf16),
             pltpu.VMEM((peers, CA, atom_count), bf16),
             pltpu.VMEM((peers, CA, atom_count), bf16),
             dma(2), dma(2), dma(p), dma(p), dma(p), dma(p), dma(r), dma(r),
@@ -479,7 +465,7 @@
         ),
         name="diffusion_block",
     )(*operands)
-    return single_out, atoms_out
+    return single_out.T, atoms_out
 
 
 def solution(mesh):

time: 72.9 us -> 60.8 us (0.83)
  Pallas kernels: 69.1 us -> 57.2 us
    pallas_call x1, Pallas kernels: 69.1 us -> 57.2 us  [body(): pl.pallas_call(functools.partial(whole_kernel, peers, rows_n), grid=(rows...]
    pallas_call x1 -> x0, local copies, waits for them, and re-layouts: 1.56 us -> none  [body(): pl.pallas_call(functools.partial(whole_kernel, peers, rows_n), grid=(rows...]
    unnamed x1 -> x2, local copies, waits for them, and re-layouts: 1.37 us -> 2.8 us
where the time goes in v7:
time: 60.8 us; the launch traced here: 60.6 us
  Pallas kernels  57.2 us (94%)
  local copies, waits for them, and re-layouts  2.8 us (5%)
  between operations  0.64 us (1%)
    pallas_call x1, Pallas kernels, body(): pl.pallas_call(functools.partial(whole_kernel, peers, rows_n), grid=(rows...  57.2 us
    unnamed x2, local copies, waits for them, and re-layouts  2.8 us

profile of v7, /device:TPU:0, one launch (start us, length us, event | category | flops | bytes accessed | tf_op | source)
XLA Modules:
  0.0 60.6 jit_solution(13037510314006110076)
XLA Ops:
  0.6 57.2 %diffusion_block.1 = (bf16[96,256]{1,0:T(8,128)(2,1)}, bf16[128,128]{1,0:T(8,128)(2,1)}) custom-call(bf16[256,128,128]{2,1,0:T(8,128)(2,1)} %pair_ref.1, bf16[128,2,256]{2,1,0:T(2,128)(2,1)} %trans_in_ref.1, bf16[256,128]{1,0:T(8,128)(2,1)} %trans_out_ref.1, bf16[16,128]{1,0:T(8,128)(2,1)} %bitcast.7, bf16[128,128]{1,0:T(8,128)(2,1)} %atoms_ref.1, ...), custom_call_target="tpu_custom_call" | custom-call | flops 7650410496 | bytes 10485760 | tf_op jit(solution)/shard_map/diffusion_block/pallas_call | solution.py:421
  57.8 1.4 %copy.19 = bf16[256,96]{0,1:T(8,128)(2,1)} copy(bf16[256,96]{0,1:T(8,128)(2,1)} %bitcast.5) | data formatting | bytes 98304
  59.2 1.4 %copy.20 = bf16[128,128]{1,0:T(8,128)(2,1)} copy(bf16[128,128]{1,0:T(8,128)(2,1)} %get-tuple-element.9) | data formatting | bytes 65536
